TPU v7x, 512 devices: a whole 4x8x8 slice. The times are simulated.
512 devices in a mesh: rows: 128 (over z, y, core), cols: 4 (over x).
Axes of the slice: x: 4, y: 8, z: 8, core: 2. Of those that a mesh axis runs over, the one named last changes fastest.
Arguments:
- right_sample: bfloat16 [32768, 320], P('rows', 'cols'), may hold values from -6 to 6
- left_sample: bfloat16 [32768, 320], P('rows', 'cols'), may hold values from -6 to 6
- updates: bfloat16 [128, 512, 512], P('rows'), may hold values from -0.25 to 0.25
- pattern: int32 [128, 4, 4], P('rows'), may hold values 0 or 1
- targets: int32 [128, 512], P('rows'), may hold values from 0 to 32767, as said below
- cluster_pos: int32 [32768], P('rows'), may hold values from 0 to 32767, as said below
- pivots: int32 [128, 128], P('rows'), may hold values from 0 to 255, as said below
Outputs:
- forward_out: float32 [32768, 320], P('rows', 'cols')
- transposed_out: float32 [32768, 320], P('rows', 'cols')
- interp: float32 [32768, 128], P('rows')
Inputs may be any that keep to these rules, and one draw needn't show every extreme that they name: `targets`: the tile rows of one index of rows name at most 6 front rows held by any one index of rows; in every draw one index of rows receives exactly 6 from every index of rows. `cluster_pos`: A permutation; the 256 front rows of one index of rows take exactly 2 positions in the block of every index of rows. The pivots of one leaf are distinct.
All inputs are finite; a program needn't handle non-finite values. No bound on the sum of `pattern` on one device may be relied on, other than what follows from the above.
Results may differ from a plain program's by a relative error of at most 0.0003.
Values may be sent and summed in bfloat16 or wider, within the bound.
No kernel may reach another device: no remote copies, remote signals or barrier semaphores. Data moves between devices by JAX's collectives and lax.ppermute only.
A program may use at most 64 MiB of HBM per device.

v0:
```python
import jax
import jax.numpy as jnp
from jax import lax
from jax.sharding import PartitionSpec as P

K = 320
LEAF = 256
RANK = 128


def per_device(right_sample, left_sample, updates, pattern, targets, cluster_pos, pivots):
    devices_rows = lax.axis_size("rows")
    children = updates.shape[0]
    block_rows = updates.shape[1]
    tile_rows = block_rows // pattern.shape[1]
    local_rows = right_sample.shape[0]
    width_half = right_sample.shape[1]
    capacity = max(2, 3 * children * block_rows // (2 * devices_rows))
    flat_rows = targets.reshape(-1)
    owner_dev = flat_rows // local_rows
    one_hot = (owner_dev[:, None] == jnp.arange(devices_rows, dtype=jnp.int32)[None, :]).astype(
        jnp.int32
    )
    rank_in = jnp.sum(jnp.cumsum(one_hot, axis=0) * one_hot, axis=1) - 1
    slot_index = owner_dev * capacity + rank_in
    requests = (
        jnp.zeros((devices_rows * capacity,), jnp.int32).at[slot_index].set(flat_rows % local_rows)
    )
    requests = requests.reshape(devices_rows, capacity)
    both_samples = jnp.concatenate([right_sample, left_sample], axis=1)
    wanted = lax.all_to_all(requests, "rows", split_axis=0, concat_axis=0, tiled=True)
    picked = both_samples[wanted]
    fetched = lax.all_to_all(picked, "rows", split_axis=0, concat_axis=0, tiled=True)
    gathered = fetched.reshape(-1, 2 * width_half)[slot_index].reshape(
        children, block_rows, 2 * width_half
    )
    mask_full = jnp.repeat(jnp.repeat(pattern, tile_rows, axis=1), tile_rows, axis=2)
    masked = jnp.where(mask_full != 0, updates, jnp.zeros_like(updates))
    forward_part = jnp.einsum(
        "cij,cjk->cik", masked, gathered[:, :, :width_half], preferred_element_type=jnp.float32
    )
    transposed_part = jnp.einsum(
        "cji,cjk->cik", masked, gathered[:, :, width_half:], preferred_element_type=jnp.float32
    )
    contrib = jnp.concatenate([forward_part, transposed_part], axis=2).reshape(-1, 2 * width_half)
    outgoing = (
        jnp.zeros((devices_rows * capacity, 2 * width_half), jnp.float32)
        .at[slot_index]
        .set(contrib)
    )
    outgoing = outgoing.reshape(devices_rows, capacity, 2 * width_half)
    incoming = lax.all_to_all(outgoing, "rows", split_axis=0, concat_axis=0, tiled=True)
    front_rows = (
        jnp.zeros((local_rows, 2 * width_half), jnp.float32)
        .at[wanted.reshape(-1)]
        .add(incoming.reshape(-1, 2 * width_half))
    )
    group_size = local_rows // devices_rows
    target_dev = cluster_pos // local_rows
    order_rows = jnp.argsort(target_dev, stable=True)
    moved_rows = front_rows[order_rows].reshape(devices_rows, group_size, 2 * width_half)
    places = (cluster_pos % local_rows)[order_rows].reshape(devices_rows, group_size)
    arrived, landing = (
        lax.all_to_all(moved_rows, "rows", split_axis=0, concat_axis=0, tiled=True),
        lax.all_to_all(places, "rows", split_axis=0, concat_axis=0, tiled=True),
    )
    clustered = (
        jnp.zeros((local_rows, 2 * width_half), jnp.float32)
        .at[landing.reshape(-1)]
        .set(arrived.reshape(-1, 2 * width_half))
    )
    leaves_dev = local_rows // LEAF
    by_leaf = clustered.reshape(leaves_dev, LEAF, 2 * width_half)
    skeleton = jnp.take_along_axis(by_leaf, pivots[:, :, None], axis=1)
    gram_part = jnp.einsum("lrk,lsk->lrs", skeleton, skeleton, precision=lax.Precision.HIGHEST)
    cross_part = jnp.einsum("lik,lsk->lis", by_leaf, skeleton, precision=lax.Precision.HIGHEST)
    gram_sum, cross_sum = lax.psum((gram_part, cross_part), "cols")
    gram = gram_sum / (2.0 * K) + jnp.eye(RANK, dtype=jnp.float32)[None]
    factor = jnp.linalg.cholesky(gram)
    solved = jax.scipy.linalg.cho_solve((factor, True), jnp.swapaxes(cross_sum / (2.0 * K), 1, 2))
    interp = jnp.swapaxes(solved, 1, 2).reshape(local_rows, RANK)
    return (clustered[:, :width_half], clustered[:, width_half:], interp)


def solution(mesh):
    return jax.shard_map(
        per_device,
        mesh=mesh,
        in_specs=(
            P("rows", "cols"),
            P("rows", "cols"),
            P("rows", None, None),
            P("rows", None, None),
            P("rows", None),
            P("rows"),
            P("rows", None),
        ),
        out_specs=(P("rows", "cols"), P("rows", "cols"), P("rows", None)),
        check_vma=False,
    )
```

profile of v0, /device:TPU:1, one launch (start us, length us, event | category | flops | bytes accessed | tf_op | source)
XLA Modules:
  0.0 227.2 jit_solution(17364629311769931984)
XLA Ops:
  9.2 2.4 %scatter_custom_fusion = s32[768]{0:T(1024)S(1)} fusion(s32[512]{0:T(512)S(1)} %bitcast.101, s32[512]{0:T(512)S(1)} %get-tuple-element.18, s32[]{:T(128)} %constant.124.clone.1), kind=kCustom, calls=%fused_computation.88 | custom fusion | bytes 3076 | tf_op jit(solution)/shard_map/scatter | solution.py:27
  12.4 18.6 %all-to-all-start.1 = ((s32[128,1,6]{2,1,0:T(1,128)}), s32[128,1,6]{2,1,0:T(1,128)S(1)}, u32[]{:S(2)}, u32[]{:S(2)}) async-start(s32[128,1,6]{2,1,0:T(1,128)} %bitcast.10), calls=%async_computation.1 | async-start | bytes 131072 | tf_op jit(solution)/shard_map/all_to_all | solution.py:31
  32.0 10.4 %all-to-all-done.1 = s32[128,1,6]{2,1,0:T(1,128)S(1)} async-done(((s32[128,1,6]{2,1,0:T(1,128)}), s32[128,1,6]{2,1,0:T(1,128)S(1)}, u32[]{:S(2)}, u32[]{:S(2)}) %all-to-all-start.1) | async-done | bytes 3104 | tf_op jit(solution)/shard_map/all_to_all | solution.py:31
  42.5 2.7 %gather_fusion.1 = bf16[768,160]{1,0:T(8,128)(2,1)S(1)} fusion(bf16[256,160]{1,0:T(8,128)(2,1)S(1)} %pad_maximum_fusion, s32[1024]{0:T(1024)S(1)} %pad_clamp_fusion.2), kind=kCustom, calls=%fused_computation.1 | custom fusion | bytes 494592 | tf_op jit(solution)/shard_map/gather | solution.py:32
  45.4 1.2 reshape.605
  46.6 5.9 %all-to-all-start.2 = ((bf16[128,2,480]{2,1,0:T(2,128)(2,1)}), bf16[128,2,480]{2,1,0:T(2,128)(2,1)S(1)}, u32[]{:S(2)}, u32[]{:S(2)}) async-start(bf16[128,2,480]{2,1,0:T(2,128)(2,1)} %reshape.605), calls=%async_computation.2 | async-start | bytes 524288 | tf_op jit(solution)/shard_map/all_to_all | solution.py:33
  52.5 1.6 broadcast_in_dim.53
  54.7 13.1 %all-to-all-done.2 = bf16[128,2,480]{2,1,0:T(2,128)(2,1)S(1)} async-done(((bf16[128,2,480]{2,1,0:T(2,128)(2,1)}), bf16[128,2,480]{2,1,0:T(2,128)(2,1)S(1)}, u32[]{:S(2)}, u32[]{:S(2)}) %all-to-all-start.2) | async-done | bytes 245792 | tf_op jit(solution)/shard_map/all_to_all | solution.py:33
  68.6 2.0 gather_fusion.2
  71.4 2.4 %scatter_custom_fusion.1 = f32[768,160]{1,0:T(8,128)S(1)} fusion(s32[512]{0:T(512)S(1)} %bitcast.103, f32[512,160]{1,0:T(8,128)S(1)} %copy.32, f32[]{:T(128)} %constant.123.clone.1), kind=kCustom, calls=%fused_computation.16 | custom fusion | bytes 491524 | tf_op jit(solution)/shard_map/scatter | solution.py:49
  74.0 2.0 reshape.607
  76.0 5.7 %all-to-all-start.3 = ((f32[128,1,960]{2,1,0:T(1,128)}), f32[128,1,960]{2,1,0:T(1,128)S(1)}, u32[]{:S(2)}, u32[]{:S(2)}) async-start(f32[128,1,960]{2,1,0:T(1,128)} %reshape.607), calls=%async_computation.3 | async-start | bytes 1048576 | tf_op jit(solution)/shard_map/all_to_all | solution.py:52
  81.7 3.2 %sort.17 = (s32[256]{0:T(256)}, s32[256]{0:T(256)S(1)}) sort(s32[256]{0:T(256)S(1)} %get-tuple-element.20, s32[256]{0:T(256)S(1)} %iota.55), dimensions={0}, to_apply=%region_0.1 | sort | flops 2048 | bytes 4096 | tf_op jit(solution)/shard_map/jit(argsort)/sort | solution.py:60
  84.9 1.9 gather_fusion
  89.1 13.3 %all-to-all-done.3 = f32[128,1,960]{2,1,0:T(1,128)S(1)} async-done(((f32[128,1,960]{2,1,0:T(1,128)}), f32[128,1,960]{2,1,0:T(1,128)S(1)}, u32[]{:S(2)}, u32[]{:S(2)}) %all-to-all-start.3) | async-done | bytes 491552 | tf_op jit(solution)/shard_map/all_to_all | solution.py:52
  102.3 5.5 %all-to-all-start = ((s32[128,1,2]{2,1,0:T(1,128)}), s32[128,1,2]{2,1,0:T(1,128)S(1)}, u32[]{:S(2)}, u32[]{:S(2)}) async-start(s32[128,1,2]{2,1,0:T(1,128)} %bitcast), calls=%async_computation | async-start | bytes 131072 | tf_op jit(solution)/shard_map/all_to_all | solution.py:65
  108.4 1.9 reduce.19
  110.8 5.6 %scatter_custom_fusion.2 = f32[256,160]{1,0:T(8,128)S(1)} fusion(s32[768]{0:T(1024)S(1)} %fusion.29, f32[768,160]{1,0:T(8,128)S(1)} %reshape.562, f32[]{:T(128)} %constant.123.clone.1), kind=kCustom, calls=%fused_computation.43 | custom fusion | flops 122880 | bytes 163844 | tf_op jit(solution)/shard_map/scatter-add | solution.py:56
  119.2 12.7 %all-to-all-start.4 = ((f32[128,2,160]{2,1,0:T(2,128)}), f32[128,2,160]{2,1,0:T(2,128)S(1)}, u32[]{:S(2)}, u32[]{:S(2)}) async-start(f32[128,2,160]{2,1,0:T(2,128)} %reshape.496), calls=%async_computation.4 | async-start | bytes 524288 | tf_op jit(solution)/shard_map/all_to_all | solution.py:64
  132.9 14.2 %all-to-all-done.4 = f32[128,2,160]{2,1,0:T(2,128)S(1)} async-done(((f32[128,2,160]{2,1,0:T(2,128)}), f32[128,2,160]{2,1,0:T(2,128)S(1)}, u32[]{:S(2)}, u32[]{:S(2)}) %all-to-all-start.4) | async-done | bytes 163872 | tf_op jit(solution)/shard_map/all_to_all | solution.py:64
  147.3 1.7 scatter_custom_fusion.3
  153.5 40.9 %all-reduce.3.cloned.1.call-done = (f32[1,256,128]{2,1,0:T(8,128)}, f32[1,128,128]{2,1,0:T(8,128)}) async-done(((f32[1,256,128]{2,1,0:T(8,128)}, f32[1,128,128]{2,1,0:T(8,128)}), (f32[1,256,128]{2,1,0:T(8,128)}, f32[1,128,128]{2,1,0:T(8,128)})) %all-reduce.3.cloned.1.call-update) | async-done | bytes 196624 | tf_op jit(solution)/shard_map/psum | solution.py:77
  196.1 11.7 %custom-call.11 = f32[1,128,128]{2,1,0:T(8,128)S(1)} custom-call(f32[1,128,128]{2,1,0:T(8,128)S(1)} %fusion.23), custom_call_target="Cholesky" | custom-call | tf_op jit(solution)/shard_map/jit(cholesky)/cholesky | solution.py:79
  209.2 9.8 %custom-call.12 = f32[1,128,128]{1,2,0:T(8,128)S(1)} custom-call(f32[1,128,128]{2,1,0:T(8,128)S(1)} %select_select_fusion), custom_call_target="InvertDiagBlocksLowerTriangular" | custom-call | tf_op jit(solution)/shard_map/jit(_cho_solve)/triangular_solve | solution.py:80
  (89 shorter events, 22.3 us)
Async XLA Ops:
  8.3 0.7 copy-start.5
  12.4 18.6 %copy-start.3 = (bf16[256,80]{0,1:T(8,128)(2,1)S(1)}, bf16[256,80]{0,1:T(8,128)(2,1)}, u32[]{:S(2)}) copy-start(bf16[256,80]{0,1:T(8,128)(2,1)} %param.8) | copy-start | bytes 122884
  12.4 29.9 %all-to-all-start.1 = ((s32[128,1,6]{2,1,0:T(1,128)}), s32[128,1,6]{2,1,0:T(1,128)S(1)}, u32[]{:S(2)}, u32[]{:S(2)}) async-start(s32[128,1,6]{2,1,0:T(1,128)} %bitcast.10), calls=%async_computation.1 | async-start | bytes 131072 | tf_op jit(solution)/shard_map/all_to_all | solution.py:31
  31.0 0.8 copy-start.4
  46.6 5.9 %copy-start.6 = (s32[1,4,4]{2,1,0:T(4,128)S(1)}, s32[1,4,4]{2,1,0:T(4,128)}, u32[]{:S(2)}) copy-start(s32[1,4,4]{2,1,0:T(4,128)} %param.10) | copy-start | bytes 196
  46.6 21.3 %all-to-all-start.2 = ((bf16[128,2,480]{2,1,0:T(2,128)(2,1)}), bf16[128,2,480]{2,1,0:T(2,128)(2,1)S(1)}, u32[]{:S(2)}, u32[]{:S(2)}) async-start(bf16[128,2,480]{2,1,0:T(2,128)(2,1)} %reshape.605), calls=%async_computation.2 | async-start | bytes 524288 | tf_op jit(solution)/shard_map/all_to_all | solution.py:33
  68.6 2.0 copy-start
  76.0 5.7 %copy-start.7 = (s32[256]{0:T(256)S(1)}, s32[256]{0:T(256)}, u32[]{:S(2)}) copy-start(s32[256]{0:T(256)} %param.12) | copy-start | bytes 3076
  76.0 26.4 %all-to-all-start.3 = ((f32[128,1,960]{2,1,0:T(1,128)}), f32[128,1,960]{2,1,0:T(1,128)S(1)}, u32[]{:S(2)}, u32[]{:S(2)}) async-start(f32[128,1,960]{2,1,0:T(1,128)} %reshape.607), calls=%async_computation.3 | async-start | bytes 1048576 | tf_op jit(solution)/shard_map/all_to_all | solution.py:52
  86.8 0.8 copy-start.8
  102.3 16.8 %all-to-all-start = ((s32[128,1,2]{2,1,0:T(1,128)}), s32[128,1,2]{2,1,0:T(1,128)S(1)}, u32[]{:S(2)}, u32[]{:S(2)}) async-start(s32[128,1,2]{2,1,0:T(1,128)} %bitcast), calls=%async_computation | async-start | bytes 131072 | tf_op jit(solution)/shard_map/all_to_all | solution.py:65
  119.2 28.0 %all-to-all-start.4 = ((f32[128,2,160]{2,1,0:T(2,128)}), f32[128,2,160]{2,1,0:T(2,128)S(1)}, u32[]{:S(2)}, u32[]{:S(2)}) async-start(f32[128,2,160]{2,1,0:T(2,128)} %reshape.496), calls=%async_computation.4 | async-start | bytes 524288 | tf_op jit(solution)/shard_map/all_to_all | solution.py:64
  131.9 62.5 %all-reduce.3.cloned.1.call-start = ((), (), s32[]{:S(2)}) async-start(), calls=%async_computation.5 | async-start | bytes 393216 | tf_op jit(solution)/shard_map/psum | solution.py:77
  195.3 0.8 copy-start.1
  196.1 22.9 %copy-start.2 = (f32[1,256,128]{2,1,0:T(8,128)S(1)}, f32[1,256,128]{2,1,0:T(8,128)}, u32[]{:S(2)}) copy-start(f32[1,256,128]{2,1,0:T(8,128)} %get-tuple-element.14) | copy-start | bytes 393220
Sparse Core Ops, SparseCore 0:
  152.1 42.2 all-reduce.2
where the time goes:
time: 229 us; the launch traced here: 227 us
  waiting for transfers between devices  92.8 us (41%)
  starting transfers between devices  48.4 us (21%)
  other arithmetic  37.4 us (16%)
  local copies, waits for them, and re-layouts  30.8 us (13%)
  between operations  14.5 us (6%)
  matrix products  3.27 us (1%)
    psum x1, waiting for transfers between devices, per_device(): gram_sum, cross_sum = lax.psum((gram_part, cross_part), 'cols')  40.9 us
    all_to_all x1, starting transfers between devices, per_device(): lax.all_to_all(requests, 'rows', split_axis=0, concat_axis=0, tiled=True)  18.6 us
    all_to_all x1, waiting for transfers between devices, per_device(): lax.all_to_all(moved_rows, 'rows', split_axis=0, concat_axis=0, tiled=True)  14.2 us
    all_to_all x1, waiting for transfers between devices, per_device(): lax.all_to_all(outgoing, 'rows', split_axis=0, concat_axis=0, tiled=True)  13.3 us
    all_to_all x1, waiting for transfers between devices, per_device(): lax.all_to_all(picked, 'rows', split_axis=0, concat_axis=0, tiled=True)  13.1 us
    all_to_all x1, starting transfers between devices, per_device(): lax.all_to_all(moved_rows, 'rows', split_axis=0, concat_axis=0, tiled=True)  12.7 us
    another operation x3, other arithmetic, per_device(): factor = jnp.linalg.cholesky(gram)  12.4 us
    another operation x2, other arithmetic, per_device(): jax.scipy.linalg.cho_solve((factor, True), jnp.swapaxes(cross_sum / (2.0...  10.5 us
  transfers between devices with their start and end apart: 6, of which 6 were waited for; matrix products, arithmetic and copies ran while one was open for 10% of the time, Pallas kernels for 0%

commit v1 on v0

v1 whole, which is shorter than its diff:
```python
import jax
import jax.numpy as jnp
from jax import lax
from jax.experimental import pallas as pl
from jax.experimental.pallas import tpu as pltpu
from jax.sharding import PartitionSpec as P

K = 320
CAP = 6
F32 = jnp.float32
BF16 = jnp.bfloat16
NT = (((1,), (1,)), ((), ()))
NN = (((1,), (0,)), ((), ()))


def mm(a, b, dims=NN):
    return lax.dot_general(a, b, dims, preferred_element_type=F32)


def iota(shape, dim):
    return lax.broadcasted_iota(jnp.int32, shape, dim)


def split3(x):
    hi = x.astype(BF16)
    rest = x - hi.astype(F32)
    mid = rest.astype(BF16)
    low = (rest - mid.astype(F32)).astype(BF16)
    return hi, mid, low


def hot(mask):
    return jnp.where(mask, 1.0, 0.0).astype(BF16)


def ranks(keys, devices):
    n = keys.shape[1]
    member = keys == iota((devices, n), 0)
    ahead = hot(iota((n, n), 0) < iota((n, n), 1))
    return member, mm(hot(member), ahead)


def pick(member, rank, slot, values):
    chosen = jnp.where(jnp.logical_and(member, rank == float(slot)), values, 0.0)
    return jnp.sum(chosen, axis=1, keepdims=True)


def request_kernel(targets_ref, pos_ref, msg_ref, rows_ref):
    devices = msg_ref.shape[0]
    lanes = iota((devices, 128), 1)
    wanted = targets_ref[...]
    member, rank = ranks(wanted >> 8, devices)
    local = ((wanted & 255) + 1).astype(F32)
    msg = jnp.zeros((devices, 128), F32)
    for slot in range(CAP):
        msg = jnp.where(lanes == slot, pick(member, rank, slot, local) - 1.0, msg)
    pos = pos_ref[...]
    member, rank = ranks(pos >> 8, devices)
    landing = (pos & 255).astype(F32)
    here = iota(pos.shape, 1).astype(F32)
    rows = jnp.zeros((devices, 128), F32)
    for slot in range(2):
        msg = jnp.where(lanes == CAP + slot, pick(member, rank, slot, landing), msg)
        rows = jnp.where(lanes == slot, pick(member, rank, slot, here), rows)
    msg_ref[...] = msg.astype(jnp.int32)
    rows_ref[...] = rows.astype(jnp.int32)


def tile_prep_kernel(targets_ref, pattern_ref, updates_ref, slots_ref, masked_ref):
    devices = slots_ref.shape[0] // CAP
    member, rank = ranks(targets_ref[...] >> 8, devices)
    for slot in range(CAP):
        slots_ref[slot * devices : (slot + 1) * devices, :] = hot(
            jnp.logical_and(member, rank == float(slot))
        )
    for a in range(4):
        for b in range(4):
            part = updates_ref[a * 128 : (a + 1) * 128, b * 128 : (b + 1) * 128]
            keep = pattern_ref[a, b] != 0
            masked_ref[a * 128 : (a + 1) * 128, b * 128 : (b + 1) * 128] = jnp.where(
                keep, part, jnp.zeros_like(part)
            )


def front_prep_kernel(recv_ref, rows_ref, move_ref, land_ref):
    devices = recv_ref.shape[0]
    recv = recv_ref[...]
    across = jnp.transpose(recv.astype(F32)).astype(jnp.int32)
    for g in range(2):
        mine = rows_ref[:, g : g + 1]
        for slot in range(CAP):
            move_ref[
                g * devices : (g + 1) * devices, slot * devices : (slot + 1) * devices
            ] = hot(mine == across[slot : slot + 1, :])
        land_ref[g * devices : (g + 1) * devices, :] = hot(
            recv[:, CAP + g : CAP + g + 1] == iota((devices, land_ref.shape[1]), 1)
        )


def put_planes(ref, slot_rows, devices):
    part = [slot_rows[s * devices : (s + 1) * devices] for s in range(CAP)]
    for s in range(CAP):
        ref[pl.ds(s, devices, stride=8), :] = part[s][:, :128]
    ref[pl.ds(6, devices, stride=8), :] = jnp.concatenate(
        [part[s][:, 128:160] for s in range(4)], axis=1
    )
    ref[pl.ds(7, devices, stride=8), :] = jnp.concatenate(
        [part[4][:, 128:160], part[5][:, 128:160], jnp.zeros((devices, 64), F32)], axis=1
    )


def reply_kernel(recv_ref, right_ref, left_ref, out_ref, scratch):
    devices = recv_ref.shape[0]
    samples = jnp.concatenate([right_ref[...], left_ref[...]], axis=0)
    places = iota((devices, samples.shape[1]), 1)
    chosen = jnp.concatenate(
        [hot(recv_ref[:, s : s + 1] == places) for s in range(CAP)], axis=0
    )
    put_planes(scratch, mm(chosen, samples, NT), devices)
    out_ref[...] = scratch[...].reshape(out_ref.shape).astype(BF16)


def tile_kernel(fetched_ref, slots_ref, masked_ref, out_ref, scratch):
    devices = fetched_ref.shape[0]
    scratch[...] = fetched_ref[...].astype(F32).reshape(scratch.shape)
    across = [
        jnp.transpose(scratch[pl.ds(s, devices, stride=8), :]) for s in range(8)
    ]
    columns = jnp.concatenate(
        [
            jnp.concatenate(
                [across[s], across[6 + s // 4][32 * (s % 4) : 32 * (s % 4) + 32]], axis=0
            )
            for s in range(CAP)
        ],
        axis=1,
    ).astype(BF16)
    slots = slots_ref[...]
    gathered = mm(columns, slots).astype(BF16)
    masked = masked_ref[...]
    half = gathered.shape[0] // 2
    forward = mm(gathered[:half], masked, NT)
    transposed = mm(gathered[half:], masked, NN)
    contrib = split3(jnp.concatenate([forward, transposed], axis=0))
    sent = mm(slots, contrib[0], NT) + mm(slots, contrib[1], NT) + mm(slots, contrib[2], NT)
    put_planes(out_ref, sent, devices)


def front_kernel(incoming_ref, move_ref, out_ref):
    devices = out_ref.shape[0]
    plane = [incoming_ref[pl.ds(s, devices, stride=8), :] for s in range(8)]
    main = split3(jnp.concatenate(plane[:CAP], axis=0))
    rest = split3(
        jnp.concatenate(
            [plane[6 + s // 4][:, 32 * (s % 4) : 32 * (s % 4) + 32] for s in range(CAP)],
            axis=0,
        )
    )
    move = move_ref[...]
    main = mm(move, main[0]) + mm(move, main[1]) + mm(move, main[2])
    rest = mm(move, rest[0]) + mm(move, rest[1]) + mm(move, rest[2])
    out_ref[:, 0:128] = main[:devices]
    out_ref[:, 128:256] = main[devices:]
    out_ref[:, 256:384] = jnp.concatenate(
        [rest[:devices], rest[devices:], jnp.zeros((devices, 64), F32)], axis=1
    )


def cluster_kernel(arrived_ref, land_ref, forward_ref, transposed_ref, joined_ref):
    first = jnp.transpose(arrived_ref[:, 0:128])
    second = jnp.transpose(arrived_ref[:, 128:256])
    rest = jnp.transpose(arrived_ref[:, 256:384])
    columns = jnp.concatenate(
        [
            jnp.concatenate([first, rest[0:32]], axis=0),
            jnp.concatenate([second, rest[32:64]], axis=0),
        ],
        axis=1,
    )
    land = land_ref[...]
    parts = split3(columns)
    joined = mm(parts[0], land) + mm(parts[1], land) + mm(parts[2], land)
    half = joined.shape[0] // 2
    forward_ref[...] = joined[:half]
    transposed_ref[...] = joined[half:]
    joined_ref[...] = joined


def mm_full(a, b):
    a0, a1, a2 = split3(a)
    b0, b1, b2 = split3(b)
    return (
        (mm(a2, b0) + mm(a1, b1) + mm(a0, b2)) + (mm(a1, b0) + mm(a0, b1))
    ) + mm(a0, b0)


def mm_hot(a, b):
    a0, a1, a2 = split3(a)
    return mm(a0, b) + mm(a1, b) + mm(a2, b)


def inverse(a):
    n = a.shape[0]
    sub, lane = iota(a.shape, 0), iota(a.shape, 1)
    for k in range(n):
        pivot = 1.0 / a[k : k + 1, k : k + 1]
        row = jnp.where(lane[k : k + 1] == k, 1.0, a[k : k + 1, :]) * pivot
        column = jnp.where(sub[:, 0:1] == k, -1.0, a[:, k : k + 1])
        rest = jnp.where(jnp.logical_or(sub == k, lane == k), 0.0, a)
        a = rest - column * row
    return a


def leaf_kernel(joined_ref, pivots_ref, interp_ref):
    joined = joined_ref[...]
    leaf, rank = joined.shape[1], pivots_ref.shape[1]
    chosen = hot(iota((leaf, rank), 0) == pivots_ref[...])
    skeleton = jnp.transpose(mm_hot(joined, chosen))
    cross = mm_full(skeleton, joined) * (1.0 / (2.0 * K))
    eye = jnp.where(iota((rank, rank), 0) == iota((rank, rank), 1), 1.0, 0.0)
    gram = mm_hot(cross, chosen) + eye
    interp_ref[...] = mm_full(jnp.transpose(cross), inverse(gram))


def call(kernel, outs, *args, scratch=(), smem=(), flops=1_000_000):
    spec = [
        pl.BlockSpec(memory_space=pltpu.SMEM if i in smem else pltpu.VMEM)
        for i in range(len(args))
    ]
    return pl.pallas_call(
        kernel,
        out_shape=outs,
        in_specs=spec,
        out_specs=jax.tree.map(lambda _: pl.BlockSpec(memory_space=pltpu.VMEM), outs),
        scratch_shapes=scratch,
        compiler_params=pltpu.CompilerParams(vmem_limit_bytes=48 * 2**20),
        cost_estimate=pl.CostEstimate(
            flops=flops, bytes_accessed=1_000_000, transcendentals=0
        ),
    )(*args)


def per_device(right_sample, left_sample, updates, pattern, targets, cluster_pos, pivots):
    devices = lax.axis_size("rows")
    local_rows, width = right_sample.shape
    block = updates.shape[1]
    shape = jax.ShapeDtypeStruct

    def exchange(x):
        return lax.all_to_all(x, "rows", split_axis=0, concat_axis=0, tiled=True)

    message, front_order = call(
        request_kernel,
        [shape((devices, 128), jnp.int32), shape((devices, 128), jnp.int32)],
        targets,
        cluster_pos.reshape(1, local_rows),
    )
    received = exchange(message)
    slots, masked = call(
        tile_prep_kernel,
        [shape((CAP * devices, block), BF16), shape((block, block), BF16)],
        targets,
        pattern[0],
        updates[0],
        smem=(1,),
    )
    reply = call(
        reply_kernel,
        shape((devices, 8, 128), BF16),
        received,
        right_sample.T,
        left_sample.T,
        scratch=[pltpu.VMEM((devices * 8, 128), F32)],
    )
    fetched = exchange(reply)
    move, land = call(
        front_prep_kernel,
        [
            shape((2 * devices, CAP * devices), BF16),
            shape((2 * devices, local_rows), BF16),
        ],
        received,
        front_order,
    )
    outgoing = call(
        tile_kernel,
        shape((devices * 8, 128), F32),
        fetched,
        slots,
        masked,
        scratch=[pltpu.VMEM((devices * 8, 128), F32)],
    )
    incoming = exchange(outgoing.reshape(devices, 8, 128)).reshape(devices * 8, 128)
    moved = call(front_kernel, shape((devices, 384), F32), incoming, move)
    arrived = exchange(moved)
    forward, transposed, joined = call(
        cluster_kernel,
        [
            shape((width, local_rows), F32),
            shape((width, local_rows), F32),
            shape((2 * width, local_rows), F32),
        ],
        arrived,
        land,
    )
    columns = lax.axis_size("cols")
    spread = lax.all_to_all(
        jnp.broadcast_to(joined[None], (columns,) + joined.shape),
        "cols",
        split_axis=0,
        concat_axis=0,
        tiled=True,
    )
    interp = call(
        leaf_kernel,
        shape((local_rows, pivots.shape[1]), F32),
        spread.reshape(columns * 2 * width, local_rows),
        pivots,
    )
    return forward.T, transposed.T, interp


def solution(mesh):
    return jax.shard_map(
        per_device,
        mesh=mesh,
        in_specs=(
            P("rows", "cols"),
            P("rows", "cols"),
            P("rows", None, None),
            P("rows", None, None),
            P("rows", None),
            P("rows"),
            P("rows", None),
        ),
        out_specs=(P("rows", "cols"), P("rows", "cols"), P("rows", None)),
        check_vma=False,
    )
```

time: 229 us -> 133 us (0.58)
  blocking collectives: 0 us -> 62.8 us
  waiting for transfers between devices: 92.8 us -> 34.1 us
  other arithmetic: 37.4 us -> 0 us
  starting transfers between devices: 48.4 us -> 11.4 us
  local copies, waits for them, and re-layouts: 30.8 us -> 2.95 us
  Pallas kernels: 0 us -> 20.2 us
  between operations: 14.5 us -> 0.76 us
  matrix products: 3.27 us -> 0 us
    all_to_all x0 -> x3, blocking collectives: none -> 62.8 us  [the longest x2 49 us: exchange(): return lax.all_to_all(x, 'rows', split_axis=0, concat_axis=0, tiled=True)]
    psum x1 -> x0, waiting for transfers between devices: 40.9 us -> none  [per_device(): gram_sum, cross_sum = lax.psum((gram_part, cross_part), 'cols')]
    all_to_all x5 -> x2, starting transfers between devices: 48.3 us -> 11.4 us  [exchange(): return lax.all_to_all(x, 'rows', split_axis=0, concat_axis=0, tiled=True)]
    another operation x8 -> x0, other arithmetic: 23.1 us -> none  [the longest x3 12.4 us: per_device(): factor = jnp.linalg.cholesky(gram)]
    pallas_call x0 -> x8, Pallas kernels: none -> 20.2 us  [call(): pl.pallas_call(kernel, out_shape=outs, in_specs=spec, out_specs=jax.tree....]
    all_to_all x5 -> x2, waiting for transfers between devices: 51.9 us -> 34.1 us  [exchange(): return lax.all_to_all(x, 'rows', split_axis=0, concat_axis=0, tiled=True)]
    gather x6 -> x0, local copies, waits for them, and re-layouts: 8.43 us -> none  [the longest x2 2.81 us: per_device(): picked = both_samples[wanted]]
    scatter x3 -> x0, local copies, waits for them, and re-layouts: 6.63 us -> none  [the longest x1 2.45 us: per_device(): jnp.zeros((devices_rows * capacity,), jnp.int32).at[slot_index]]
  transfers between devices with their start and end apart: 6 -> 2, of which waited for: 6 -> 2; matrix products, arithmetic and copies ran while one was open for 10% -> 0% of each run, Pallas kernels for 0% -> 1%
where the time goes in v1:
time: 133 us; the launch traced here: 132 us
  blocking collectives  62.8 us (47%)
  waiting for transfers between devices  34.1 us (26%)
  Pallas kernels  20.2 us (15%)
  starting transfers between devices  11.4 us (9%)
  local copies, waits for them, and re-layouts  2.95 us (2%)
    all_to_all x2, blocking collectives, exchange(): return lax.all_to_all(x, 'rows', split_axis=0, concat_axis=0, tiled=True)  49 us
    all_to_all x2, waiting for transfers between devices, exchange(): return lax.all_to_all(x, 'rows', split_axis=0, concat_axis=0, tiled=True)  34.1 us
    pallas_call x8, Pallas kernels, call(): pl.pallas_call(kernel, out_shape=outs, in_specs=spec, out_specs=jax.tree....  20.2 us
    all_to_all x1, blocking collectives, per_device(): lax.all_to_all(jnp.broadcast_to(joined[None], (columns,) + joined.shape),...  13.8 us
    all_to_all x2, starting transfers between devices, exchange(): return lax.all_to_all(x, 'rows', split_axis=0, concat_axis=0, tiled=True)  11.4 us
    unnamed x17, local copies, waits for them, and re-layouts  2.7 us
  transfers between devices with their start and end apart: 2, of which 2 were waited for; matrix products, arithmetic and copies ran while one was open for 0% of the time, Pallas kernels for 1%

profile of v1, /device:TPU:1, one launch (start us, length us, event | category | flops | bytes accessed | tf_op | source)
XLA Modules:
  0.0 132.3 jit_solution(18129442180804179524)
XLA Ops:
  0.6 0.7 copy-done.7
  1.3 0.7 copy-done.3
  2.0 0.5 shard_map.94
  2.5 0.0 copy-start.1
  2.5 0.0 copy-start.2
  2.5 0.0 copy-start
  2.6 29.8 %all_to_all.37 = s32[128,1,128]{2,1,0:T(1,128)S(1)} all-to-all(s32[128,1,128]{2,1,0:T(1,128)S(1)} %bitcast.25), channel_id=1, replica_groups=mesh['rows'=128,'cols'=4] {'rows'}, dimensions={0} | all-to-all | bytes 131072 | tf_op jit(solution)/shard_map/all_to_all | solution.py:250
  32.4 1.1 shard_map.95
  33.5 5.9 %all-to-all-start.1 = ((bf16[128,8,128]{2,1,0:T(8,128)(2,1)}), bf16[128,8,128]{2,1,0:T(8,128)(2,1)S(1)}, u32[]{:S(2)}, u32[]{:S(2)}) async-start(bf16[128,8,128]{2,1,0:T(8,128)(2,1)} %shard_map.95), calls=%async_computation.1 | async-start | bytes 524288 | tf_op jit(solution)/shard_map/all_to_all | solution.py:250
  39.4 0.0 copy-start.4
  39.4 0.7 copy-done.4
  40.1 1.1 shard_map.96
  41.1 13.6 %all-to-all-done.1.fetched_ref = bf16[128,8,128]{2,1,0:T(8,128)(2,1)S(1)} async-done(((bf16[128,8,128]{2,1,0:T(8,128)(2,1)}), bf16[128,8,128]{2,1,0:T(8,128)(2,1)S(1)}, u32[]{:S(2)}, u32[]{:S(2)}) %all-to-all-start.1) | async-done | bytes 262176 | tf_op jit(solution)/shard_map/all_to_all | solution.py:250
  54.8 2.3 %shard_map.97 = f32[1024,128]{1,0:T(8,128)} custom-call(bf16[128,8,128]{2,1,0:T(8,128)(2,1)S(1)} %all-to-all-done.1.fetched_ref, bf16[768,512]{1,0:T(8,128)(2,1)S(1)} %get-tuple-element.13.slots_ref, bf16[512,512]{1,0:T(8,128)(2,1)S(1)} %get-tuple-element.14.masked_ref), custom_call_target="tpu_custom_call" | custom-call | flops 1000000 | bytes 1000000 | tf_op jit(solution)/shard_map/pallas_call | solution.py:230
  57.0 5.5 %all-to-all-start.2 = ((f32[128,8,128]{2,1,0:T(8,128)}), f32[128,8,128]{2,1,0:T(8,128)S(1)}, u32[]{:S(2)}, u32[]{:S(2)}) async-start(f32[128,8,128]{2,1,0:T(8,128)} %bitcast.8), calls=%async_computation.2 | async-start | bytes 1048576 | tf_op jit(solution)/shard_map/all_to_all | solution.py:250
  62.5 0.2 shard_map.98
  62.7 20.5 %all-to-all-done.2 = f32[128,8,128]{2,1,0:T(8,128)S(1)} async-done(((f32[128,8,128]{2,1,0:T(8,128)}), f32[128,8,128]{2,1,0:T(8,128)S(1)}, u32[]{:S(2)}, u32[]{:S(2)}) %all-to-all-start.2) | async-done | bytes 524320 | tf_op jit(solution)/shard_map/all_to_all | solution.py:250
  83.2 0.9 shard_map.99
  84.1 0.2 copy.11
  84.3 19.2 %all_to_all.38 = f32[128,1,384]{2,1,0:T(1,128)S(1)} all-to-all(f32[128,1,384]{2,1,0:T(1,128)S(1)} %copy.11), channel_id=1, replica_groups=mesh['rows'=128,'cols'=4] {'rows'}, dimensions={0} | all-to-all | bytes 393216 | tf_op jit(solution)/shard_map/all_to_all | solution.py:250
  103.5 0.9 shard_map.100
  104.5 13.8 %all_to_all.39 = f32[4,160,256]{2,1,0:T(8,128)S(1)} all-to-all(f32[4,160,256]{2,1,0:T(8,128)S(1)} %broadcast_in_dim.2), channel_id=1, replica_groups=mesh['rows'=128,'cols'=4] {'cols'}, dimensions={0} | all-to-all | bytes 1310720 | tf_op jit(solution)/shard_map/all_to_all | solution.py:307
  118.3 0.7 copy-done.6
  119.0 13.3 %shard_map.101 = f32[256,128]{1,0:T(8,128)} custom-call(f32[640,256]{1,0:T(8,128)S(1)} %bitcast.18, s32[1,128]{1,0:T(1,128)S(1)} %copy-done.6), custom_call_target="tpu_custom_call" | custom-call | flops 1000000 | bytes 1000000 | tf_op jit(solution)/shard_map/pallas_call | solution.py:230
  (10 shorter events, 0.1 us)
Async XLA Ops:
  0.6 0.7 copy-start.7
  1.3 0.7 copy-start.3
  2.5 29.8 %copy-start.1 = (bf16[256,80]{0,1:T(8,128)(2,1)S(1)}, bf16[256,80]{0,1:T(8,128)(2,1)}, u32[]{:S(2)}) copy-start(bf16[256,80]{0,1:T(8,128)(2,1)} %param.7) | copy-start | bytes 122884
  2.5 29.8 %copy-start.2 = (bf16[256,80]{0,1:T(8,128)(2,1)S(1)}, bf16[256,80]{0,1:T(8,128)(2,1)}, u32[]{:S(2)}) copy-start(bf16[256,80]{0,1:T(8,128)(2,1)} %param.8) | copy-start | bytes 122884
  2.5 36.9 %copy-start = (bf16[1,512,512]{2,1,0:T(8,128)(2,1)S(1)}, bf16[1,512,512]{2,1,0:T(8,128)(2,1)}, u32[]{:S(2)}) copy-start(bf16[1,512,512]{2,1,0:T(8,128)(2,1)} %param.9) | copy-start | bytes 1572868
  33.5 5.9 %copy-start.5 = (s32[1,4,4]{2,1,0:T(4,128)S(1)}, s32[1,4,4]{2,1,0:T(4,128)}, u32[]{:S(2)}) copy-start(s32[1,4,4]{2,1,0:T(4,128)} %param.10) | copy-start | bytes 196
  33.5 21.2 %all-to-all-start.1 = ((bf16[128,8,128]{2,1,0:T(8,128)(2,1)}), bf16[128,8,128]{2,1,0:T(8,128)(2,1)S(1)}, u32[]{:S(2)}, u32[]{:S(2)}) async-start(bf16[128,8,128]{2,1,0:T(8,128)(2,1)} %shard_map.95), calls=%async_computation.1 | async-start | bytes 524288 | tf_op jit(solution)/shard_map/all_to_all | solution.py:250
  39.4 0.7 copy-start.4
  57.0 26.2 %all-to-all-start.2 = ((f32[128,8,128]{2,1,0:T(8,128)}), f32[128,8,128]{2,1,0:T(8,128)S(1)}, u32[]{:S(2)}, u32[]{:S(2)}) async-start(f32[128,8,128]{2,1,0:T(8,128)} %bitcast.8), calls=%async_computation.2 | async-start | bytes 1048576 | tf_op jit(solution)/shard_map/all_to_all | solution.py:250
  118.3 0.7 copy-start.6

commit v2 on v1

--- a/solution.py
+++ b/solution.py
@@ -7,6 +7,9 @@
 
 K = 320
 CAP = 6
+HALF = 80
+CODES = 64
+LOG2 = 0.6931471805599453
 F32 = jnp.float32
 BF16 = jnp.bfloat16
 NT = (((1,), (1,)), ((), ()))
@@ -45,8 +48,16 @@
     return jnp.sum(chosen, axis=1, keepdims=True)
 
 
-def request_kernel(targets_ref, pos_ref, msg_ref, rows_ref):
+def request_kernel(
+    targets_hbm, pos_hbm, msg_ref, rows_ref, targets_ref, pos_ref, arrivals
+):
     devices = msg_ref.shape[0]
+    first = pltpu.make_async_copy(targets_hbm, targets_ref, arrivals.at[0])
+    second = pltpu.make_async_copy(pos_hbm, pos_ref, arrivals.at[1])
+    first.start()
+    second.start()
+    first.wait()
+    second.wait()
     lanes = iota((devices, 128), 1)
     wanted = targets_ref[...]
     member, rank = ranks(wanted >> 8, devices)
@@ -66,9 +77,15 @@
     rows_ref[...] = rows.astype(jnp.int32)
 
 
-def tile_prep_kernel(targets_ref, pattern_ref, updates_ref, slots_ref, masked_ref):
-    devices = slots_ref.shape[0] // CAP
+def tile_prep_kernel(
+    targets_ref, pattern_ref, updates_ref, slots_ref, member_ref, rank_ref, masked_ref
+):
+    devices = member_ref.shape[0]
     member, rank = ranks(targets_ref[...] >> 8, devices)
+    member_ref[...] = hot(member)
+    rank_ref[...] = jnp.broadcast_to(
+        jnp.sum(jnp.where(member, rank, 0.0), axis=0, keepdims=True), rank_ref.shape
+    )
     for slot in range(CAP):
         slots_ref[slot * devices : (slot + 1) * devices, :] = hot(
             jnp.logical_and(member, rank == float(slot))
@@ -82,7 +99,9 @@
             )
 
 
-def front_prep_kernel(recv_ref, rows_ref, move_ref, land_ref):
+def front_prep_kernel(
+    recv_ref, rows_ref, pivots_ref, move_ref, land_ref, scale_ref, chosen_ref
+):
     devices = recv_ref.shape[0]
     recv = recv_ref[...]
     across = jnp.transpose(recv.astype(F32)).astype(jnp.int32)
@@ -95,18 +114,16 @@
         land_ref[g * devices : (g + 1) * devices, :] = hot(
             recv[:, CAP + g : CAP + g + 1] == iota((devices, land_ref.shape[1]), 1)
         )
-
-
-def put_planes(ref, slot_rows, devices):
-    part = [slot_rows[s * devices : (s + 1) * devices] for s in range(CAP)]
+    place, lane = iota((128, 128), 0), iota((128, 128), 1)
     for s in range(CAP):
-        ref[pl.ds(s, devices, stride=8), :] = part[s][:, :128]
-    ref[pl.ds(6, devices, stride=8), :] = jnp.concatenate(
-        [part[s][:, 128:160] for s in range(4)], axis=1
-    )
-    ref[pl.ds(7, devices, stride=8), :] = jnp.concatenate(
-        [part[4][:, 128:160], part[5][:, 128:160], jnp.zeros((devices, 64), F32)], axis=1
-    )
+        scale_ref[:, 128 * s : 128 * s + 128] = hot(
+            place == CODES + s + jnp.where(lane >= HALF, 8, 0)
+        )
+    for s in (6, 7):
+        scale_ref[:, 128 * s : 128 * s + 128] = hot(
+            place == CODES + 8 + 4 * (s - 6) + (lane >> 5)
+        )
+    chosen_ref[...] = hot(iota(chosen_ref.shape, 0) == pivots_ref[...])
 
 
 def reply_kernel(recv_ref, right_ref, left_ref, out_ref, scratch):
@@ -116,39 +133,85 @@
     chosen = jnp.concatenate(
         [hot(recv_ref[:, s : s + 1] == places) for s in range(CAP)], axis=0
     )
-    put_planes(scratch, mm(chosen, samples, NT), devices)
+    rows = mm(chosen, samples, NT)
+    part = [rows[s * devices : (s + 1) * devices] for s in range(CAP)]
+    for s in range(CAP):
+        scratch[pl.ds(s, devices, stride=8), :] = part[s][:, :128]
+    scratch[pl.ds(6, devices, stride=8), :] = jnp.concatenate(
+        [part[s][:, 128:160] for s in range(4)], axis=1
+    )
+    scratch[pl.ds(7, devices, stride=8), :] = jnp.concatenate(
+        [part[4][:, 128:160], part[5][:, 128:160], jnp.zeros((devices, 64), F32)], axis=1
+    )
     out_ref[...] = scratch[...].reshape(out_ref.shape).astype(BF16)
 
 
-def tile_kernel(fetched_ref, slots_ref, masked_ref, out_ref, scratch):
-    devices = fetched_ref.shape[0]
+def steps_of(code):
+    return jnp.exp(code * (LOG2 / 256.0)) * (1.0 / 32600.0)
+
+
+def coded(x):
+    peak = jnp.maximum(jnp.max(jnp.abs(x), axis=0, keepdims=True), 1e-32)
+    code = jnp.ceil(jnp.log(peak) * (256.0 / LOG2))
+    return jnp.floor(x / steps_of(code) + 0.5), code
+
+
+def mm_whole(hots, x):
+    high = jnp.floor(x * (1.0 / 256.0) + 0.5)
+    low = x - 256.0 * high
+    return mm(hots, high.astype(BF16), NT) * 256.0 + mm(hots, low.astype(BF16), NT)
+
+
+def tile_kernel(
+    fetched_ref, slots_ref, member_ref, rank_ref, masked_ref, out_ref, scratch
+):
+    devices, columns = member_ref.shape
     scratch[...] = fetched_ref[...].astype(F32).reshape(scratch.shape)
     across = [
-        jnp.transpose(scratch[pl.ds(s, devices, stride=8), :]) for s in range(8)
+        jnp.transpose(scratch[pl.ds(s, devices, stride=8), :]).astype(BF16)
+        for s in range(8)
     ]
-    columns = jnp.concatenate(
-        [
-            jnp.concatenate(
-                [across[s], across[6 + s // 4][32 * (s % 4) : 32 * (s % 4) + 32]], axis=0
-            )
-            for s in range(CAP)
-        ],
-        axis=1,
-    ).astype(BF16)
-    slots = slots_ref[...]
-    gathered = mm(columns, slots).astype(BF16)
+    slots, member, rank = slots_ref[...], member_ref[...], rank_ref[0:1, :]
+    main = mm(jnp.concatenate(across[:CAP], axis=1), slots)
+    rest = mm(jnp.concatenate(across[CAP:], axis=0), member)
+    tail = jnp.zeros((32, columns), F32)
+    for s in range(CAP):
+        tail = jnp.where(rank == float(s), rest[32 * s : 32 * s + 32], tail)
+    gathered = jnp.concatenate([main, tail], axis=0).astype(BF16)
     masked = masked_ref[...]
-    half = gathered.shape[0] // 2
-    forward = mm(gathered[:half], masked, NT)
-    transposed = mm(gathered[half:], masked, NN)
-    contrib = split3(jnp.concatenate([forward, transposed], axis=0))
-    sent = mm(slots, contrib[0], NT) + mm(slots, contrib[1], NT) + mm(slots, contrib[2], NT)
-    put_planes(out_ref, sent, devices)
-
-
-def front_kernel(incoming_ref, move_ref, out_ref):
+    forward, forward_code = coded(mm(gathered[:HALF], masked, NT))
+    transposed, transposed_code = coded(mm(gathered[HALF:], masked, NN))
+    tail = transposed[128 - HALF :]
+    row = iota((8, columns), 0).astype(F32)
+    rest = jnp.concatenate(
+        [jnp.where(rank == float(s), tail, 0.0) for s in range(CAP)]
+        + [
+            jnp.where(rank == row, forward_code, 0.0),
+            jnp.where(rank == row, transposed_code, 0.0),
+            jnp.zeros((48, columns), F32),
+        ],
+        axis=0,
+    )
+    main = mm_whole(slots, jnp.concatenate([forward, transposed[: 128 - HALF]], axis=0))
+    rest = mm_whole(member, rest)
+    for s in range(CAP):
+        scratch[pl.ds(s, devices, stride=8), :] = main[s * devices : (s + 1) * devices]
+    scratch[pl.ds(6, devices, stride=8), :] = rest[:, :128]
+    scratch[pl.ds(7, devices, stride=8), :] = rest[:, 128:]
+    out_ref[...] = (
+        scratch[...].reshape(out_ref.shape).astype(jnp.int32).astype(jnp.int16)
+    )
+
+
+def front_kernel(incoming_ref, move_ref, scale_ref, out_ref, scratch):
     devices = out_ref.shape[0]
-    plane = [incoming_ref[pl.ds(s, devices, stride=8), :] for s in range(8)]
+    scratch[...] = (
+        incoming_ref[...].astype(jnp.int32).astype(F32).reshape(scratch.shape)
+    )
+    plane = [scratch[pl.ds(s, devices, stride=8), :] for s in range(8)]
+    codes = jnp.where(iota(plane[7].shape, 1) >= CODES, plane[7], 0.0)
+    scales = mm_hot(steps_of(codes), scale_ref[...])
+    plane = [plane[s] * scales[:, 128 * s : 128 * s + 128] for s in range(8)]
     main = split3(jnp.concatenate(plane[:CAP], axis=0))
     rest = split3(
         jnp.concatenate(
@@ -199,22 +262,89 @@
     return mm(a0, b) + mm(a1, b) + mm(a2, b)
 
 
-def inverse(a):
-    n = a.shape[0]
-    sub, lane = iota(a.shape, 0), iota(a.shape, 1)
-    for k in range(n):
-        pivot = 1.0 / a[k : k + 1, k : k + 1]
-        row = jnp.where(lane[k : k + 1] == k, 1.0, a[k : k + 1, :]) * pivot
-        column = jnp.where(sub[:, 0:1] == k, -1.0, a[:, k : k + 1])
-        rest = jnp.where(jnp.logical_or(sub == k, lane == k), 0.0, a)
-        a = rest - column * row
-    return a
-
-
-def leaf_kernel(joined_ref, pivots_ref, interp_ref):
-    joined = joined_ref[...]
-    leaf, rank = joined.shape[1], pivots_ref.shape[1]
-    chosen = hot(iota((leaf, rank), 0) == pivots_ref[...])
+def small_inverse(p, n):
+    def at(d, i, j):
+        return d[min(i, j), max(i, j)]
+
+    if n == 1:
+        return {(0, 0): 1.0 / p[0, 0]}
+    if n == 2:
+        a, b, c = p[0, 0], p[0, 1], p[1, 1]
+        r = 1.0 / (a * c - b * b)
+        return {(0, 0): c * r, (0, 1): -b * r, (1, 1): a * r}
+    h = n // 2
+    pairs = [(i, j) for i in range(h) for j in range(i, h)]
+    first = small_inverse({(i, j): p[i, j] for i, j in pairs}, h)
+    w = {
+        (i, j): sum(at(first, i, k) * p[k, h + j] for k in range(h))
+        for i in range(h)
+        for j in range(h)
+    }
+    second = small_inverse(
+        {
+            (i, j): p[h + i, h + j] - sum(p[k, h + i] * w[k, j] for k in range(h))
+            for i, j in pairs
+        },
+        h,
+    )
+    t = {
+        (i, j): sum(w[i, k] * at(second, k, j) for k in range(h))
+        for i in range(h)
+        for j in range(h)
+    }
+    out = {(i, h + j): -t[i, j] for i in range(h) for j in range(h)}
+    for i, j in pairs:
+        out[i, j] = first[i, j] + sum(t[i, k] * w[j, k] for k in range(h))
+        out[h + i, h + j] = second[i, j]
+    return out
+
+
+def inverse(matrix, b=4):
+    n = matrix.shape[0]
+    a = [matrix[8 * i : 8 * i + 8] for i in range(n // 8)]
+    shape = a[0].shape
+    sub, lane = iota(shape, 0), iota(shape, 1)
+
+    def spread(x):
+        return jnp.broadcast_to(x, shape)
+
+    for k in range(0, n, b):
+        group, o = divmod(k, 8)
+        rows = [spread(a[group][o + q : o + q + 1, :]) for q in range(b)]
+        pivot = small_inverse(
+            {
+                (q, r): spread(rows[q][:, k + r : k + r + 1])
+                for q in range(b)
+                for r in range(q, b)
+            },
+            b,
+        )
+        inside = jnp.logical_and(lane >= k, lane < k + b)
+        rows = [
+            jnp.where(inside, jnp.where(lane == k + q, 1.0, 0.0), rows[q])
+            for q in range(b)
+        ]
+        new = [
+            sum(pivot[min(q, r), max(q, r)] * rows[r] for r in range(b))
+            for q in range(b)
+        ]
+        mine = jnp.logical_and(sub >= o, sub < o + b)
+        for i in range(n // 8):
+            total = jnp.where(inside, 0.0, a[i])
+            for q in range(b):
+                total = total - spread(a[i][:, k + q : k + q + 1]) * new[q]
+            if i == group:
+                picked = new[0]
+                for q in range(1, b):
+                    picked = jnp.where(sub == o + q, new[q], picked)
+                total = jnp.where(mine, picked, total)
+            a[i] = total
+    return jnp.concatenate(a, axis=0)
+
+
+def leaf_kernel(joined_ref, chosen_ref, interp_ref):
+    joined, chosen = joined_ref[...], chosen_ref[...]
+    rank = chosen.shape[1]
     skeleton = jnp.transpose(mm_hot(joined, chosen))
     cross = mm_full(skeleton, joined) * (1.0 / (2.0 * K))
     eye = jnp.where(iota((rank, rank), 0) == iota((rank, rank), 1), 1.0, 0.0)
@@ -222,9 +352,11 @@
     interp_ref[...] = mm_full(jnp.transpose(cross), inverse(gram))
 
 
-def call(kernel, outs, *args, scratch=(), smem=(), flops=1_000_000):
+def call(kernel, outs, *args, scratch=(), smem=(), hbm=(), flops=1_000_000):
     spec = [
-        pl.BlockSpec(memory_space=pltpu.SMEM if i in smem else pltpu.VMEM)
+        pl.BlockSpec(
+            memory_space=pltpu.SMEM if i in smem else pltpu.HBM if i in hbm else pltpu.VMEM
+        )
         for i in range(len(args))
     ]
     return pl.pallas_call(
@@ -254,11 +386,22 @@
         [shape((devices, 128), jnp.int32), shape((devices, 128), jnp.int32)],
         targets,
         cluster_pos.reshape(1, local_rows),
+        hbm=(0, 1),
+        scratch=[
+            pltpu.VMEM((1, block), jnp.int32),
+            pltpu.VMEM((1, local_rows), jnp.int32),
+            pltpu.SemaphoreType.DMA((2,)),
+        ],
     )
     received = exchange(message)
-    slots, masked = call(
+    slots, member, rank, masked = call(
         tile_prep_kernel,
-        [shape((CAP * devices, block), BF16), shape((block, block), BF16)],
+        [
+            shape((CAP * devices, block), BF16),
+            shape((devices, block), BF16),
+            shape((8, block), F32),
+            shape((block, block), BF16),
+        ],
         targets,
         pattern[0],
         updates[0],
@@ -273,25 +416,37 @@
         scratch=[pltpu.VMEM((devices * 8, 128), F32)],
     )
     fetched = exchange(reply)
-    move, land = call(
+    move, land, scale, chosen = call(
         front_prep_kernel,
         [
             shape((2 * devices, CAP * devices), BF16),
             shape((2 * devices, local_rows), BF16),
+            shape((128, 1024), BF16),
+            shape((local_rows, pivots.shape[1]), BF16),
         ],
         received,
         front_order,
+        pivots,
     )
     outgoing = call(
         tile_kernel,
-        shape((devices * 8, 128), F32),
+        shape((devices, 8, 128), jnp.int16),
         fetched,
         slots,
+        member,
+        rank,
         masked,
         scratch=[pltpu.VMEM((devices * 8, 128), F32)],
     )
-    incoming = exchange(outgoing.reshape(devices, 8, 128)).reshape(devices * 8, 128)
-    moved = call(front_kernel, shape((devices, 384), F32), incoming, move)
+    incoming = exchange(outgoing)
+    moved = call(
+        front_kernel,
+        shape((devices, 384), F32),
+        incoming,
+        move,
+        scale,
+        scratch=[pltpu.VMEM((devices * 8, 128), F32)],
+    )
     arrived = exchange(moved)
     forward, transposed, joined = call(
         cluster_kernel,
@@ -315,7 +470,7 @@
         leaf_kernel,
         shape((local_rows, pivots.shape[1]), F32),
         spread.reshape(columns * 2 * width, local_rows),
-        pivots,
+        chosen,
     )
     return forward.T, transposed.T, interp
 

time: 133 us -> 122 us (0.917)
  waiting for transfers between devices: 34.1 us -> 28 us
  Pallas kernels: 20.2 us -> 15.7 us
    all_to_all x2, waiting for transfers between devices: 34.1 us -> 28 us  [exchange(): return lax.all_to_all(x, 'rows', split_axis=0, concat_axis=0, tiled=True)]
    pallas_call x8, Pallas kernels: 20.2 us -> 15.7 us  [call(): pl.pallas_call(kernel, out_shape=outs, in_specs=spec, out_specs=jax.tree....]
where the time goes in v2:
time: 122 us; the launch traced here: 121 us
  blocking collectives  62.6 us (51%)
  waiting for transfers between devices  28 us (23%)
  Pallas kernels  15.7 us (13%)
  starting transfers between devices  11.4 us (9%)
  local copies, waits for them, and re-layouts  2.94 us (2%)
    all_to_all x2, blocking collectives, exchange(): return lax.all_to_all(x, 'rows', split_axis=0, concat_axis=0, tiled=True)  48.8 us
    all_to_all x2, waiting for transfers between devices, exchange(): return lax.all_to_all(x, 'rows', split_axis=0, concat_axis=0, tiled=True)  28 us
    pallas_call x8, Pallas kernels, call(): pl.pallas_call(kernel, out_shape=outs, in_specs=spec, out_specs=jax.tree....  15.7 us
    all_to_all x1, blocking collectives, per_device(): lax.all_to_all(jnp.broadcast_to(joined[None], (columns,) + joined.shape),...  13.8 us
    all_to_all x2, starting transfers between devices, exchange(): return lax.all_to_all(x, 'rows', split_axis=0, concat_axis=0, tiled=True)  11.4 us
    unnamed x17, local copies, waits for them, and re-layouts  2.7 us
  transfers between devices with their start and end apart: 2, of which 2 were waited for; matrix products, arithmetic and copies ran while one was open for 0% of the time, Pallas kernels for 1%

profile of v2, /device:TPU:1, one launch (start us, length us, event | category | flops | bytes accessed | tf_op | source)
XLA Modules:
  0.0 121.4 jit_solution(4828909702399475249)
XLA Ops:
  0.6 0.7 copy-done.7
  1.3 0.7 copy-done.3
  2.0 0.5 shard_map.94
  2.5 0.0 copy-start.1
  2.6 0.0 copy-start.2
  2.6 0.0 copy-start
  2.6 29.8 %all_to_all.37 = s32[128,1,128]{2,1,0:T(1,128)S(1)} all-to-all(s32[128,1,128]{2,1,0:T(1,128)S(1)} %bitcast.22), channel_id=1, replica_groups=mesh['rows'=128,'cols'=4] {'rows'}, dimensions={0} | all-to-all | bytes 131072 | tf_op jit(solution)/shard_map/all_to_all | solution.py:382
  32.4 1.1 shard_map.95
  33.5 5.9 %all-to-all-start.1 = ((bf16[128,8,128]{2,1,0:T(8,128)(2,1)}), bf16[128,8,128]{2,1,0:T(8,128)(2,1)S(1)}, u32[]{:S(2)}, u32[]{:S(2)}) async-start(bf16[128,8,128]{2,1,0:T(8,128)(2,1)} %shard_map.95), calls=%async_computation.1 | async-start | bytes 524288 | tf_op jit(solution)/shard_map/all_to_all | solution.py:382
  39.4 0.0 copy-start.4
  39.4 0.7 copy-done.4
  40.1 1.1 shard_map.96
  41.2 13.6 %all-to-all-done.1.fetched_ref = bf16[128,8,128]{2,1,0:T(8,128)(2,1)S(1)} async-done(((bf16[128,8,128]{2,1,0:T(8,128)(2,1)}), bf16[128,8,128]{2,1,0:T(8,128)(2,1)S(1)}, u32[]{:S(2)}, u32[]{:S(2)}) %all-to-all-start.1) | async-done | bytes 262176 | tf_op jit(solution)/shard_map/all_to_all | solution.py:382
  54.8 2.1 %shard_map.97 = s16[128,8,128]{2,1,0:T(8,128)(2,1)} custom-call(bf16[128,8,128]{2,1,0:T(8,128)(2,1)S(1)} %all-to-all-done.1.fetched_ref, bf16[768,512]{1,0:T(8,128)(2,1)S(1)} %get-tuple-element.17.slots_ref, bf16[128,512]{1,0:T(8,128)(2,1)S(1)} %get-tuple-element.18.member_ref, f32[8,512]{1,0:T(8,128)S(1)} %get-tuple-element.19.rank_ref, ...), custom_call_target="tpu_custom_call" | custom-call | flops 1000000 | bytes 1000000 | tf_op jit(solution)/shard_map/pallas_call | solution.py:362
  56.8 5.5 %all-to-all-start.2 = ((s16[128,8,128]{2,1,0:T(8,128)(2,1)}), s16[128,8,128]{2,1,0:T(8,128)(2,1)S(1)}, u32[]{:S(2)}, u32[]{:S(2)}) async-start(s16[128,8,128]{2,1,0:T(8,128)(2,1)} %shard_map.97), calls=%async_computation.2 | async-start | bytes 524288 | tf_op jit(solution)/shard_map/all_to_all | solution.py:382
  62.4 0.6 copy-done.6
  63.0 0.2 shard_map.98
  63.3 14.5 %all-to-all-done.2.incoming_ref = s16[128,8,128]{2,1,0:T(8,128)(2,1)S(1)} async-done(((s16[128,8,128]{2,1,0:T(8,128)(2,1)}), s16[128,8,128]{2,1,0:T(8,128)(2,1)S(1)}, u32[]{:S(2)}, u32[]{:S(2)}) %all-to-all-start.2) | async-done | bytes 262176 | tf_op jit(solution)/shard_map/all_to_all | solution.py:382
  77.7 1.2 shard_map.99
  78.9 0.2 copy.11
  79.2 19.0 %all_to_all.38 = f32[128,1,384]{2,1,0:T(1,128)S(1)} all-to-all(f32[128,1,384]{2,1,0:T(1,128)S(1)} %copy.11), channel_id=1, replica_groups=mesh['rows'=128,'cols'=4] {'rows'}, dimensions={0} | all-to-all | bytes 393216 | tf_op jit(solution)/shard_map/all_to_all | solution.py:382
  98.1 0.9 shard_map.100
  99.1 13.8 %all_to_all.39 = f32[4,160,256]{2,1,0:T(8,128)S(1)} all-to-all(f32[4,160,256]{2,1,0:T(8,128)S(1)} %broadcast_in_dim.2), channel_id=1, replica_groups=mesh['rows'=128,'cols'=4] {'cols'}, dimensions={0} | all-to-all | bytes 1310720 | tf_op jit(solution)/shard_map/all_to_all | solution.py:462
  112.9 8.5 %shard_map.101 = f32[256,128]{1,0:T(8,128)} custom-call(f32[640,256]{1,0:T(8,128)S(1)} %bitcast.16, bf16[256,128]{1,0:T(8,128)(2,1)S(1)} %get-tuple-element.28.chosen_ref), custom_call_target="tpu_custom_call" | custom-call | flops 1000000 | bytes 1000000 | tf_op jit(solution)/shard_map/pallas_call | solution.py:362
  (10 shorter events, 0.1 us)
Async XLA Ops:
  0.6 0.7 copy-start.7
  1.3 0.7 copy-start.3
  2.5 29.8 %copy-start.1 = (bf16[256,80]{0,1:T(8,128)(2,1)S(1)}, bf16[256,80]{0,1:T(8,128)(2,1)}, u32[]{:S(2)}) copy-start(bf16[256,80]{0,1:T(8,128)(2,1)} %param.7) | copy-start | bytes 122884
  2.6 29.8 %copy-start.2 = (bf16[256,80]{0,1:T(8,128)(2,1)S(1)}, bf16[256,80]{0,1:T(8,128)(2,1)}, u32[]{:S(2)}) copy-start(bf16[256,80]{0,1:T(8,128)(2,1)} %param.8) | copy-start | bytes 122884
  2.6 36.9 %copy-start = (bf16[1,512,512]{2,1,0:T(8,128)(2,1)S(1)}, bf16[1,512,512]{2,1,0:T(8,128)(2,1)}, u32[]{:S(2)}) copy-start(bf16[1,512,512]{2,1,0:T(8,128)(2,1)} %param.9) | copy-start | bytes 1572868
  33.5 5.9 %copy-start.5 = (s32[1,4,4]{2,1,0:T(4,128)S(1)}, s32[1,4,4]{2,1,0:T(4,128)}, u32[]{:S(2)}) copy-start(s32[1,4,4]{2,1,0:T(4,128)} %param.10) | copy-start | bytes 196
  33.5 21.2 %all-to-all-start.1 = ((bf16[128,8,128]{2,1,0:T(8,128)(2,1)}), bf16[128,8,128]{2,1,0:T(8,128)(2,1)S(1)}, u32[]{:S(2)}, u32[]{:S(2)}) async-start(bf16[128,8,128]{2,1,0:T(8,128)(2,1)} %shard_map.95), calls=%async_computation.1 | async-start | bytes 524288 | tf_op jit(solution)/shard_map/all_to_all | solution.py:382
  39.4 0.7 copy-start.4
  56.8 20.9 %all-to-all-start.2 = ((s16[128,8,128]{2,1,0:T(8,128)(2,1)}), s16[128,8,128]{2,1,0:T(8,128)(2,1)S(1)}, u32[]{:S(2)}, u32[]{:S(2)}) async-start(s16[128,8,128]{2,1,0:T(8,128)(2,1)} %shard_map.97), calls=%async_computation.2 | async-start | bytes 524288 | tf_op jit(solution)/shard_map/all_to_all | solution.py:382
  62.4 0.7 copy-start.6

commit v3 on v2

--- a/solution.py
+++ b/solution.py
@@ -100,9 +100,10 @@
 
 
 def front_prep_kernel(
-    recv_ref, rows_ref, pivots_ref, move_ref, land_ref, scale_ref, chosen_ref
+    recv_ref, rows_ref, pivots_ref, move_ref, land_ref, leaf_land_ref, scale_ref, order_ref
 ):
     devices = recv_ref.shape[0]
+    leaf, rank = land_ref.shape[1], pivots_ref.shape[1]
     recv = recv_ref[...]
     across = jnp.transpose(recv.astype(F32)).astype(jnp.int32)
     for g in range(2):
@@ -112,8 +113,17 @@
                 g * devices : (g + 1) * devices, slot * devices : (slot + 1) * devices
             ] = hot(mine == across[slot : slot + 1, :])
         land_ref[g * devices : (g + 1) * devices, :] = hot(
-            recv[:, CAP + g : CAP + g + 1] == iota((devices, land_ref.shape[1]), 1)
+            recv[:, CAP + g : CAP + g + 1] == iota((devices, leaf), 1)
         )
+    pivot = iota((leaf, rank), 0) == pivots_ref[...]
+    other = 1.0 - jnp.sum(jnp.where(pivot, 1.0, 0.0), axis=1, keepdims=True)
+    other = jnp.broadcast_to(other, (leaf, leaf - rank))
+    ahead = mm(hot(iota((leaf, leaf), 1) < iota((leaf, leaf), 0)), other.astype(BF16))
+    order_ref[:, :rank] = hot(pivot)
+    order_ref[:, rank:] = hot(
+        jnp.logical_and(other > 0.5, ahead == iota(ahead.shape, 1).astype(F32))
+    )
+    leaf_land_ref[...] = jnp.transpose(mm(land_ref[...], order_ref[...])).astype(BF16)
     place, lane = iota((128, 128), 0), iota((128, 128), 1)
     for s in range(CAP):
         scale_ref[:, 128 * s : 128 * s + 128] = hot(
@@ -123,8 +133,6 @@
         scale_ref[:, 128 * s : 128 * s + 128] = hot(
             place == CODES + 8 + 4 * (s - 6) + (lane >> 5)
         )
-    chosen_ref[...] = hot(iota(chosen_ref.shape, 0) == pivots_ref[...])
-
 
 def reply_kernel(recv_ref, right_ref, left_ref, out_ref, scratch):
     devices = recv_ref.shape[0]
@@ -229,7 +237,26 @@
     )
 
 
-def cluster_kernel(arrived_ref, land_ref, forward_ref, transposed_ref, joined_ref):
+def mm_split(hots, x):
+    x0, x1, x2 = split3(x)
+    return mm(hots, x0) + mm(hots, x1) + mm(hots, x2)
+
+
+def pack_kernel(arrived_ref, leaf_land_ref, out_ref):
+    land = leaf_land_ref[...]
+    rest = arrived_ref[:, 256:384]
+    main = mm_split(
+        land, jnp.concatenate([arrived_ref[:, 0:128], arrived_ref[:, 128:256]], axis=0)
+    )
+    rest = mm_split(land, jnp.concatenate([rest[:, 0:32], rest[:, 32:64]], axis=0))
+    leaf = main.shape[0]
+    out_ref[:leaf] = main
+    out_ref[leaf:] = jnp.concatenate(
+        [rest[leaf // 4 * k : leaf // 4 * (k + 1)] for k in range(4)], axis=1
+    )
+
+
+def cluster_kernel(arrived_ref, land_ref, forward_ref, transposed_ref):
     first = jnp.transpose(arrived_ref[:, 0:128])
     second = jnp.transpose(arrived_ref[:, 128:256])
     rest = jnp.transpose(arrived_ref[:, 256:384])
@@ -240,21 +267,16 @@
         ],
         axis=1,
     )
-    land = land_ref[...]
-    parts = split3(columns)
-    joined = mm(parts[0], land) + mm(parts[1], land) + mm(parts[2], land)
-    half = joined.shape[0] // 2
-    forward_ref[...] = joined[:half]
-    transposed_ref[...] = joined[half:]
-    joined_ref[...] = joined
-
-
-def mm_full(a, b):
-    a0, a1, a2 = split3(a)
-    b0, b1, b2 = split3(b)
-    return (
-        (mm(a2, b0) + mm(a1, b1) + mm(a0, b2)) + (mm(a1, b0) + mm(a0, b1))
-    ) + mm(a0, b0)
+    joined = mm_hot(columns, land_ref[...])
+    forward_ref[...] = joined[:HALF]
+    transposed_ref[...] = joined[HALF:]
+
+
+def mm_full(a, b, dims=NN):
+    a0, a1, a2 = a
+    b0, b1, b2 = b
+    small = mm(a2, b0, dims) + mm(a1, b1, dims) + mm(a0, b2, dims)
+    return (small + (mm(a1, b0, dims) + mm(a0, b1, dims))) + mm(a0, b0, dims)
 
 
 def mm_hot(a, b):
@@ -262,94 +284,94 @@
     return mm(a0, b) + mm(a1, b) + mm(a2, b)
 
 
-def small_inverse(p, n):
-    def at(d, i, j):
-        return d[min(i, j), max(i, j)]
-
-    if n == 1:
-        return {(0, 0): 1.0 / p[0, 0]}
-    if n == 2:
-        a, b, c = p[0, 0], p[0, 1], p[1, 1]
-        r = 1.0 / (a * c - b * b)
-        return {(0, 0): c * r, (0, 1): -b * r, (1, 1): a * r}
-    h = n // 2
-    pairs = [(i, j) for i in range(h) for j in range(i, h)]
-    first = small_inverse({(i, j): p[i, j] for i, j in pairs}, h)
-    w = {
-        (i, j): sum(at(first, i, k) * p[k, h + j] for k in range(h))
-        for i in range(h)
-        for j in range(h)
-    }
-    second = small_inverse(
-        {
-            (i, j): p[h + i, h + j] - sum(p[k, h + i] * w[k, j] for k in range(h))
-            for i, j in pairs
-        },
-        h,
-    )
-    t = {
-        (i, j): sum(w[i, k] * at(second, k, j) for k in range(h))
-        for i in range(h)
-        for j in range(h)
-    }
-    out = {(i, h + j): -t[i, j] for i in range(h) for j in range(h)}
-    for i, j in pairs:
-        out[i, j] = first[i, j] + sum(t[i, k] * w[j, k] for k in range(h))
-        out[h + i, h + j] = second[i, j]
-    return out
-
-
-def inverse(matrix, b=4):
-    n = matrix.shape[0]
-    a = [matrix[8 * i : 8 * i + 8] for i in range(n // 8)]
+def small_solve(p, rows):
+    n = len(rows)
+    p, rows, w, scaled = dict(p), list(rows), {}, []
+    for i in range(0, n, 2):
+        j = i + 1
+        a, h, c = p[i, i], p[i, j], p[j, j]
+        r = 1.0 / (a * c - h * h)
+        aa, hh, cc = c * r, -(h * r), a * r
+        later = range(j + 1, n)
+        for m in later:
+            w[i, m] = aa * p[i, m] + hh * p[j, m]
+            w[j, m] = hh * p[i, m] + cc * p[j, m]
+        for m in later:
+            for q in range(m, n):
+                p[m, q] = p[m, q] - (p[i, m] * w[i, q] + p[j, m] * w[j, q])
+        for m in later:
+            rows[m] = rows[m] - (w[i, m] * rows[i] + w[j, m] * rows[j])
+        scaled.append(aa * rows[i] + hh * rows[j])
+        scaled.append(hh * rows[i] + cc * rows[j])
+    for i in range(n - 4, -1, -2):
+        for q in (i, i + 1):
+            for m in range(i + 2, n, 2):
+                scaled[q] = scaled[q] - (w[q, m] * scaled[m] + w[q, m + 1] * scaled[m + 1])
+    return scaled
+
+
+def inverse(matrix):
+    n, b = matrix.shape[0], 8
+    a = [matrix[b * i : b * i + b] for i in range(n // b)]
     shape = a[0].shape
     sub, lane = iota(shape, 0), iota(shape, 1)
+    lower, solved = [], []
 
     def spread(x):
         return jnp.broadcast_to(x, shape)
 
-    for k in range(0, n, b):
-        group, o = divmod(k, 8)
-        rows = [spread(a[group][o + q : o + q + 1, :]) for q in range(b)]
-        pivot = small_inverse(
-            {
-                (q, r): spread(rows[q][:, k + r : k + r + 1])
-                for q in range(b)
-                for r in range(q, b)
-            },
-            b,
-        )
+    for g in range(n // b):
+        k = b * g
+        rows = [spread(a[g][q : q + 1, :]) for q in range(b)]
+        p = {
+            (q, r): spread(rows[q][:, k + r : k + r + 1])
+            for q in range(b)
+            for r in range(q, b)
+        }
         inside = jnp.logical_and(lane >= k, lane < k + b)
         rows = [
             jnp.where(inside, jnp.where(lane == k + q, 1.0, 0.0), rows[q])
             for q in range(b)
         ]
-        new = [
-            sum(pivot[min(q, r), max(q, r)] * rows[r] for r in range(b))
-            for q in range(b)
-        ]
-        mine = jnp.logical_and(sub >= o, sub < o + b)
-        for i in range(n // 8):
-            total = jnp.where(inside, 0.0, a[i])
-            for q in range(b):
-                total = total - spread(a[i][:, k + q : k + q + 1]) * new[q]
-            if i == group:
-                picked = new[0]
-                for q in range(1, b):
-                    picked = jnp.where(sub == o + q, new[q], picked)
-                total = jnp.where(mine, picked, total)
-            a[i] = total
-    return jnp.concatenate(a, axis=0)
-
-
-def leaf_kernel(joined_ref, chosen_ref, interp_ref):
-    joined, chosen = joined_ref[...], chosen_ref[...]
-    rank = chosen.shape[1]
-    skeleton = jnp.transpose(mm_hot(joined, chosen))
-    cross = mm_full(skeleton, joined) * (1.0 / (2.0 * K))
+        new = small_solve(p, rows)
+        left, picked = rows[0], new[0]
+        for q in range(1, b):
+            left = jnp.where(sub == q, rows[q], left)
+            picked = jnp.where(sub == q, new[q], picked)
+        lower.append(jnp.where(lane < k + b, left, 0.0))
+        solved.append(jnp.where(lane < k + b, picked, 0.0))
+        for i in range(g + 1, n // b):
+            terms = [spread(a[i][:, k + q : k + q + 1]) * new[q] for q in range(b)]
+            while len(terms) > 1:
+                terms = [terms[t] + terms[t + 1] for t in range(0, len(terms), 2)]
+            a[i] = jnp.where(inside, 0.0, a[i]) - terms[0]
+    lower = jnp.transpose(jnp.concatenate(lower, axis=0))
+    return mm_full(split3(lower), split3(jnp.concatenate(solved, axis=0)))
+
+
+def leaf_kernel(spread_ref, order_ref, interp_ref):
+    columns = spread_ref.shape[0]
+    leaf, rank = interp_ref.shape
+    quarter = leaf // 4
+    rest = [spread_ref[c, leaf:, :] for c in range(columns)]
+    rest = jnp.concatenate(
+        [
+            jnp.concatenate([x[:, 32 * k : 32 * k + 32] for x in rest], axis=1)
+            for k in range(4)
+        ],
+        axis=0,
+    )
+    rows = split3(
+        jnp.concatenate([spread_ref[c, :leaf, :] for c in range(columns)] + [rest], axis=1)
+    )
+    pivots = [part[:rank] for part in rows]
+    others = [part[rank:] for part in rows]
     eye = jnp.where(iota((rank, rank), 0) == iota((rank, rank), 1), 1.0, 0.0)
-    gram = mm_hot(cross, chosen) + eye
-    interp_ref[...] = mm_full(jnp.transpose(cross), inverse(gram))
+    gram = mm_full(pivots, pivots, NT) * (1.0 / (2.0 * K)) + eye
+    cross = mm_full(others, pivots, NT) * (1.0 / (2.0 * K))
+    chosen = order_ref[:, :rank].astype(F32)
+    cross = split3(mm_split(order_ref[:, rank:], cross) - chosen)
+    interp_ref[...] = chosen + mm_full(cross, split3(inverse(gram)))
 
 
 def call(kernel, outs, *args, scratch=(), smem=(), hbm=(), flops=1_000_000):
@@ -384,8 +406,8 @@
     message, front_order = call(
         request_kernel,
         [shape((devices, 128), jnp.int32), shape((devices, 128), jnp.int32)],
-        targets,
-        cluster_pos.reshape(1, local_rows),
+        pltpu.with_memory_space_constraint(targets, pltpu.HBM),
+        pltpu.with_memory_space_constraint(cluster_pos.reshape(1, local_rows), pltpu.HBM),
         hbm=(0, 1),
         scratch=[
             pltpu.VMEM((1, block), jnp.int32),
@@ -416,13 +438,14 @@
         scratch=[pltpu.VMEM((devices * 8, 128), F32)],
     )
     fetched = exchange(reply)
-    move, land, scale, chosen = call(
+    move, land, leaf_land, scale, order = call(
         front_prep_kernel,
         [
             shape((2 * devices, CAP * devices), BF16),
             shape((2 * devices, local_rows), BF16),
+            shape((local_rows, 2 * devices), BF16),
             shape((128, 1024), BF16),
-            shape((local_rows, pivots.shape[1]), BF16),
+            shape((local_rows, local_rows), BF16),
         ],
         received,
         front_order,
@@ -448,29 +471,25 @@
         scratch=[pltpu.VMEM((devices * 8, 128), F32)],
     )
     arrived = exchange(moved)
-    forward, transposed, joined = call(
-        cluster_kernel,
-        [
-            shape((width, local_rows), F32),
-            shape((width, local_rows), F32),
-            shape((2 * width, local_rows), F32),
-        ],
-        arrived,
-        land,
+    packed = call(
+        pack_kernel, shape((local_rows * 5 // 4, 128), F32), arrived, leaf_land
     )
     columns = lax.axis_size("cols")
     spread = lax.all_to_all(
-        jnp.broadcast_to(joined[None], (columns,) + joined.shape),
+        jnp.broadcast_to(packed[None], (columns,) + packed.shape),
         "cols",
         split_axis=0,
         concat_axis=0,
         tiled=True,
     )
+    forward, transposed = call(
+        cluster_kernel,
+        [shape((width, local_rows), F32), shape((width, local_rows), F32)],
+        arrived,
+        land,
+    )
     interp = call(
-        leaf_kernel,
-        shape((local_rows, pivots.shape[1]), F32),
-        spread.reshape(columns * 2 * width, local_rows),
-        chosen,
+        leaf_kernel, shape((local_rows, pivots.shape[1]), F32), spread, order
     )
     return forward.T, transposed.T, interp
 

time: 122 us -> 120 us (0.984)
  blocking collectives: 62.6 us -> 48.8 us
  waiting for transfers between devices: 28 us -> 37.1 us
  starting transfers between devices: 11.4 us -> 15.4 us
    all_to_all x1 -> x0, blocking collectives: 13.8 us -> none  [per_device(): lax.all_to_all(jnp.broadcast_to(joined[None], (columns,) + joined.shape),...]
    all_to_all x0 -> x1, waiting for transfers between devices: none -> 9.34 us  [per_device(): lax.all_to_all(jnp.broadcast_to(packed[None], (columns,) + packed.shape),...]
    all_to_all x0 -> x1, starting transfers between devices: none -> 4.01 us  [per_device(): lax.all_to_all(jnp.broadcast_to(packed[None], (columns,) + packed.shape),...]
    unnamed x17 -> x13, local copies, waits for them, and re-layouts: 2.7 us -> 1.34 us
    pallas_call x8 -> x9, Pallas kernels: 15.7 us -> 15.3 us  [call(): pl.pallas_call(kernel, out_shape=outs, in_specs=spec, out_specs=jax.tree....]
  transfers between devices with their start and end apart: 2 -> 3, of which waited for: 2 -> 3; matrix products, arithmetic and copies ran while one was open for 0% -> 0% of each run, Pallas kernels for 1% -> 2%
where the time goes in v3:
time: 120 us
  blocking collectives  48.8 us (41%)
  waiting for transfers between devices  37.1 us (31%)
  starting transfers between devices  15.4 us (13%)
  Pallas kernels  15.3 us (13%)
  local copies, waits for them, and re-layouts  2.44 us (2%)
    all_to_all x2, blocking collectives, exchange(): return lax.all_to_all(x, 'rows', split_axis=0, concat_axis=0, tiled=True)  48.8 us
    all_to_all x2, waiting for transfers between devices, exchange(): return lax.all_to_all(x, 'rows', split_axis=0, concat_axis=0, tiled=True)  27.7 us
    pallas_call x9, Pallas kernels, call(): pl.pallas_call(kernel, out_shape=outs, in_specs=spec, out_specs=jax.tree....  15.3 us
    all_to_all x2, starting transfers between devices, exchange(): return lax.all_to_all(x, 'rows', split_axis=0, concat_axis=0, tiled=True)  11.4 us
    all_to_all x1, waiting for transfers between devices, per_device(): lax.all_to_all(jnp.broadcast_to(packed[None], (columns,) + packed.shape),...  9.34 us
    all_to_all x1, starting transfers between devices, per_device(): lax.all_to_all(jnp.broadcast_to(packed[None], (columns,) + packed.shape),...  4.01 us
  transfers between devices with their start and end apart: 3, of which 3 were waited for; matrix products, arithmetic and copies ran while one was open for 0% of the time, Pallas kernels for 2%

profile of v3, /device:TPU:1, one launch (start us, length us, event | category | flops | bytes accessed | tf_op | source)
XLA Modules:
  0.0 119.7 jit_solution(1713718866565744121)
XLA Ops:
  0.6 1.2 %shard_map.94 = (s32[128,128]{1,0:T(8,128)S(1)}, s32[128,128]{1,0:T(8,128)S(1)}) custom-call(s32[1,512]{1,0:T(1,128)} %targets_ref.1, s32[1,256]{1,0:T(1,128)} %bitcast.27), custom_call_target="tpu_custom_call" | custom-call | flops 1000000 | bytes 1000000 | tf_op jit(solution)/shard_map/pallas_call | solution.py:384
  1.9 0.0 copy-start
  1.9 29.8 %all_to_all.37 = s32[128,1,128]{2,1,0:T(1,128)S(1)} all-to-all(s32[128,1,128]{2,1,0:T(1,128)S(1)} %bitcast.21), channel_id=1, replica_groups=mesh['rows'=128,'cols'=4] {'rows'}, dimensions={0} | all-to-all | bytes 131072 | tf_op jit(solution)/shard_map/all_to_all | solution.py:404
  31.7 1.1 shard_map.95
  32.9 5.9 %all-to-all-start.1 = ((bf16[128,8,128]{2,1,0:T(8,128)(2,1)}), bf16[128,8,128]{2,1,0:T(8,128)(2,1)S(1)}, u32[]{:S(2)}, u32[]{:S(2)}) async-start(bf16[128,8,128]{2,1,0:T(8,128)(2,1)} %shard_map.95), calls=%async_computation.1 | async-start | bytes 524288 | tf_op jit(solution)/shard_map/all_to_all | solution.py:404
  38.7 0.0 copy-start.3
  38.8 0.7 copy-done.3
  39.4 1.1 shard_map.96
  40.5 13.6 %all-to-all-done.1.fetched_ref = bf16[128,8,128]{2,1,0:T(8,128)(2,1)S(1)} async-done(((bf16[128,8,128]{2,1,0:T(8,128)(2,1)}), bf16[128,8,128]{2,1,0:T(8,128)(2,1)S(1)}, u32[]{:S(2)}, u32[]{:S(2)}) %all-to-all-start.1) | async-done | bytes 262176 | tf_op jit(solution)/shard_map/all_to_all | solution.py:404
  54.1 2.1 %shard_map.97 = s16[128,8,128]{2,1,0:T(8,128)(2,1)} custom-call(bf16[128,8,128]{2,1,0:T(8,128)(2,1)S(1)} %all-to-all-done.1.fetched_ref, bf16[768,512]{1,0:T(8,128)(2,1)S(1)} %get-tuple-element.17.slots_ref, bf16[128,512]{1,0:T(8,128)(2,1)S(1)} %get-tuple-element.18.member_ref, f32[8,512]{1,0:T(8,128)S(1)} %get-tuple-element.19.rank_ref, ...), custom_call_target="tpu_custom_call" | custom-call | flops 1000000 | bytes 1000000 | tf_op jit(solution)/shard_map/pallas_call | solution.py:384
  56.2 5.5 %all-to-all-start.2 = ((s16[128,8,128]{2,1,0:T(8,128)(2,1)}), s16[128,8,128]{2,1,0:T(8,128)(2,1)S(1)}, u32[]{:S(2)}, u32[]{:S(2)}) async-start(s16[128,8,128]{2,1,0:T(8,128)(2,1)} %shard_map.97), calls=%async_computation.2 | async-start | bytes 524288 | tf_op jit(solution)/shard_map/all_to_all | solution.py:404
  61.7 0.0 copy-start.5
  61.7 0.6 copy-done.5
  62.4 0.6 shard_map.98
  62.9 14.1 %all-to-all-done.2.incoming_ref = s16[128,8,128]{2,1,0:T(8,128)(2,1)S(1)} async-done(((s16[128,8,128]{2,1,0:T(8,128)(2,1)}), s16[128,8,128]{2,1,0:T(8,128)(2,1)S(1)}, u32[]{:S(2)}, u32[]{:S(2)}) %all-to-all-start.2) | async-done | bytes 262176 | tf_op jit(solution)/shard_map/all_to_all | solution.py:404
  77.1 1.2 %shard_map.99 = f32[128,384]{1,0:T(8,128)S(1)} custom-call(s16[128,8,128]{2,1,0:T(8,128)(2,1)S(1)} %all-to-all-done.2.incoming_ref, bf16[256,768]{1,0:T(8,128)(2,1)S(1)} %get-tuple-element.22.move_ref, bf16[128,1024]{1,0:T(8,128)(2,1)S(1)} %get-tuple-element.23.scale_ref), custom_call_target="tpu_custom_call" | custom-call | flops 1000000 | bytes 1000000 | tf_op jit(solution)/shard_map/pallas_call | solution.py:384
  78.3 0.2 copy.11
  78.5 19.0 %all_to_all.38 = f32[128,1,384]{2,1,0:T(1,128)S(1)} all-to-all(f32[128,1,384]{2,1,0:T(1,128)S(1)} %copy.11), channel_id=1, replica_groups=mesh['rows'=128,'cols'=4] {'rows'}, dimensions={0} | all-to-all | bytes 393216 | tf_op jit(solution)/shard_map/all_to_all | solution.py:404
  97.5 0.4 shard_map.101
  97.9 0.9 broadcast_in_dim.2
  98.8 4.0 %all-to-all-start.4 = ((f32[4,320,128]{2,1,0:T(8,128)}), f32[4,320,128]{2,1,0:T(8,128)S(1)}, u32[]{:S(2)}, u32[]{:S(2)}) async-start(f32[4,320,128]{2,1,0:T(8,128)} %broadcast_in_dim.2), calls=%async_computation.4 | async-start | bytes 1310720 | tf_op jit(solution)/shard_map/all_to_all | solution.py:478
  102.8 0.9 shard_map.100
  103.8 9.3 %all-to-all-done.4.spread_ref = f32[4,320,128]{2,1,0:T(8,128)S(1)} async-done(((f32[4,320,128]{2,1,0:T(8,128)}), f32[4,320,128]{2,1,0:T(8,128)S(1)}, u32[]{:S(2)}, u32[]{:S(2)}) %all-to-all-start.4) | async-done | bytes 655392 | tf_op jit(solution)/shard_map/all_to_all | solution.py:478
  113.1 6.6 %shard_map.102 = f32[256,128]{1,0:T(8,128)} custom-call(f32[4,320,128]{2,1,0:T(8,128)S(1)} %all-to-all-done.4.spread_ref, bf16[256,256]{1,0:T(8,128)(2,1)S(1)} %get-tuple-element.28.order_ref), custom_call_target="tpu_custom_call" | custom-call | flops 1000000 | bytes 1000000 | tf_op jit(solution)/shard_map/pallas_call | solution.py:384
  (8 shorter events, 0.0 us)
Async XLA Ops:
  1.9 29.8 %copy-start.1 = (bf16[256,80]{0,1:T(8,128)(2,1)S(1)}, bf16[256,80]{0,1:T(8,128)(2,1)}, u32[]{:S(2)}) copy-start(bf16[256,80]{0,1:T(8,128)(2,1)} %param.7) | copy-start | bytes 122884
  1.9 29.8 %copy-start.2 = (bf16[256,80]{0,1:T(8,128)(2,1)S(1)}, bf16[256,80]{0,1:T(8,128)(2,1)}, u32[]{:S(2)}) copy-start(bf16[256,80]{0,1:T(8,128)(2,1)} %param.8) | copy-start | bytes 122884
  1.9 36.9 %copy-start = (bf16[1,512,512]{2,1,0:T(8,128)(2,1)S(1)}, bf16[1,512,512]{2,1,0:T(8,128)(2,1)}, u32[]{:S(2)}) copy-start(bf16[1,512,512]{2,1,0:T(8,128)(2,1)} %param.9) | copy-start | bytes 1572868
  32.9 5.9 %copy-start.4 = (s32[1,4,4]{2,1,0:T(4,128)S(1)}, s32[1,4,4]{2,1,0:T(4,128)}, u32[]{:S(2)}) copy-start(s32[1,4,4]{2,1,0:T(4,128)} %param.10) | copy-start | bytes 196
  32.9 21.2 %all-to-all-start.1 = ((bf16[128,8,128]{2,1,0:T(8,128)(2,1)}), bf16[128,8,128]{2,1,0:T(8,128)(2,1)S(1)}, u32[]{:S(2)}, u32[]{:S(2)}) async-start(bf16[128,8,128]{2,1,0:T(8,128)(2,1)} %shard_map.95), calls=%async_computation.1 | async-start | bytes 524288 | tf_op jit(solution)/shard_map/all_to_all | solution.py:404
  38.7 0.7 copy-start.3
  56.2 20.9 %all-to-all-start.2 = ((s16[128,8,128]{2,1,0:T(8,128)(2,1)}), s16[128,8,128]{2,1,0:T(8,128)(2,1)S(1)}, u32[]{:S(2)}, u32[]{:S(2)}) async-start(s16[128,8,128]{2,1,0:T(8,128)(2,1)} %shard_map.97), calls=%async_computation.2 | async-start | bytes 524288 | tf_op jit(solution)/shard_map/all_to_all | solution.py:404
  61.7 0.7 copy-start.5
  98.8 14.3 %all-to-all-start.4 = ((f32[4,320,128]{2,1,0:T(8,128)}), f32[4,320,128]{2,1,0:T(8,128)S(1)}, u32[]{:S(2)}, u32[]{:S(2)}) async-start(f32[4,320,128]{2,1,0:T(8,128)} %broadcast_in_dim.2), calls=%async_computation.4 | async-start | bytes 1310720 | tf_op jit(solution)/shard_map/all_to_all | solution.py:478

commit v4 on v3

--- a/solution.py
+++ b/solution.py
@@ -48,9 +48,7 @@
     return jnp.sum(chosen, axis=1, keepdims=True)
 
 
-def request_kernel(
-    targets_hbm, pos_hbm, msg_ref, rows_ref, targets_ref, pos_ref, arrivals
-):
+def request_kernel(targets_hbm, pos_hbm, msg_ref, targets_ref, pos_ref, arrivals):
     devices = msg_ref.shape[0]
     first = pltpu.make_async_copy(targets_hbm, targets_ref, arrivals.at[0])
     second = pltpu.make_async_copy(pos_hbm, pos_ref, arrivals.at[1])
@@ -68,17 +66,25 @@
     pos = pos_ref[...]
     member, rank = ranks(pos >> 8, devices)
     landing = (pos & 255).astype(F32)
-    here = iota(pos.shape, 1).astype(F32)
-    rows = jnp.zeros((devices, 128), F32)
     for slot in range(2):
         msg = jnp.where(lanes == CAP + slot, pick(member, rank, slot, landing), msg)
-        rows = jnp.where(lanes == slot, pick(member, rank, slot, here), rows)
     msg_ref[...] = msg.astype(jnp.int32)
-    rows_ref[...] = rows.astype(jnp.int32)
-
-
-def tile_prep_kernel(
-    targets_ref, pattern_ref, updates_ref, slots_ref, member_ref, rank_ref, masked_ref
+
+
+def prep_kernel(
+    targets_ref,
+    pattern_ref,
+    updates_ref,
+    pos_ref,
+    pivots_ref,
+    slots_ref,
+    member_ref,
+    rank_ref,
+    masked_ref,
+    rows_ref,
+    order_ref,
+    index_ref,
+    scale_ref,
 ):
     devices = member_ref.shape[0]
     member, rank = ranks(targets_ref[...] >> 8, devices)
@@ -97,34 +103,27 @@
             masked_ref[a * 128 : (a + 1) * 128, b * 128 : (b + 1) * 128] = jnp.where(
                 keep, part, jnp.zeros_like(part)
             )
-
-
-def front_prep_kernel(
-    recv_ref, rows_ref, pivots_ref, move_ref, land_ref, leaf_land_ref, scale_ref, order_ref
-):
-    devices = recv_ref.shape[0]
-    leaf, rank = land_ref.shape[1], pivots_ref.shape[1]
-    recv = recv_ref[...]
-    across = jnp.transpose(recv.astype(F32)).astype(jnp.int32)
-    for g in range(2):
-        mine = rows_ref[:, g : g + 1]
-        for slot in range(CAP):
-            move_ref[
-                g * devices : (g + 1) * devices, slot * devices : (slot + 1) * devices
-            ] = hot(mine == across[slot : slot + 1, :])
-        land_ref[g * devices : (g + 1) * devices, :] = hot(
-            recv[:, CAP + g : CAP + g + 1] == iota((devices, leaf), 1)
-        )
-    pivot = iota((leaf, rank), 0) == pivots_ref[...]
+    pos = pos_ref[...]
+    member, rank = ranks(pos >> 8, devices)
+    here = iota(pos.shape, 1).astype(F32)
+    place, lane = iota((128, 128), 0), iota((128, 128), 1)
+    rows = jnp.zeros(rows_ref.shape, F32)
+    for slot in range(2):
+        rows = jnp.where(lane == slot, pick(member, rank, slot, here), rows)
+    rows_ref[...] = rows.astype(jnp.int32)
+    leaf, count = order_ref.shape[0], pivots_ref.shape[1]
+    pivot = iota((leaf, count), 0) == pivots_ref[...]
     other = 1.0 - jnp.sum(jnp.where(pivot, 1.0, 0.0), axis=1, keepdims=True)
-    other = jnp.broadcast_to(other, (leaf, leaf - rank))
+    other = jnp.broadcast_to(other, (leaf, leaf - count))
     ahead = mm(hot(iota((leaf, leaf), 1) < iota((leaf, leaf), 0)), other.astype(BF16))
-    order_ref[:, :rank] = hot(pivot)
-    order_ref[:, rank:] = hot(
+    order_ref[:, :count] = hot(pivot)
+    order_ref[:, count:] = hot(
         jnp.logical_and(other > 0.5, ahead == iota(ahead.shape, 1).astype(F32))
     )
-    leaf_land_ref[...] = jnp.transpose(mm(land_ref[...], order_ref[...])).astype(BF16)
-    place, lane = iota((128, 128), 0), iota((128, 128), 1)
+    place_of = jnp.where(order_ref[...] > 0.5, iota((leaf, leaf), 1).astype(F32), 0.0)
+    index_ref[...] = jnp.broadcast_to(
+        jnp.sum(place_of, axis=1, keepdims=True), index_ref.shape
+    )
     for s in range(CAP):
         scale_ref[:, 128 * s : 128 * s + 128] = hot(
             place == CODES + s + jnp.where(lane >= HALF, 8, 0)
@@ -133,6 +132,7 @@
         scale_ref[:, 128 * s : 128 * s + 128] = hot(
             place == CODES + 8 + 4 * (s - 6) + (lane >> 5)
         )
+
 
 def reply_kernel(recv_ref, right_ref, left_ref, out_ref, scratch):
     devices = recv_ref.shape[0]
@@ -211,8 +211,22 @@
     )
 
 
-def front_kernel(incoming_ref, move_ref, scale_ref, out_ref, scratch):
+def front_kernel(incoming_ref, recv_ref, rows_ref, scale_ref, out_ref, scratch):
     devices = out_ref.shape[0]
+    across = jnp.transpose(recv_ref[...].astype(F32)).astype(jnp.int32)
+    move = jnp.concatenate(
+        [
+            jnp.concatenate(
+                [
+                    hot(rows_ref[:, g : g + 1] == across[s : s + 1, :])
+                    for s in range(CAP)
+                ],
+                axis=1,
+            )
+            for g in range(2)
+        ],
+        axis=0,
+    )
     scratch[...] = (
         incoming_ref[...].astype(jnp.int32).astype(F32).reshape(scratch.shape)
     )
@@ -227,7 +241,6 @@
             axis=0,
         )
     )
-    move = move_ref[...]
     main = mm(move, main[0]) + mm(move, main[1]) + mm(move, main[2])
     rest = mm(move, rest[0]) + mm(move, rest[1]) + mm(move, rest[2])
     out_ref[:, 0:128] = main[:devices]
@@ -242,21 +255,37 @@
     return mm(hots, x0) + mm(hots, x1) + mm(hots, x2)
 
 
-def pack_kernel(arrived_ref, leaf_land_ref, out_ref):
-    land = leaf_land_ref[...]
+def pack_kernel(arrived_ref, recv_ref, index_ref, out_ref):
+    leaf = index_ref.shape[0]
+    across = jnp.transpose(recv_ref[...].astype(F32))
+    landing = jnp.concatenate([across[CAP : CAP + 1], across[CAP + 1 : CAP + 2]], axis=1)
+    row = iota((leaf, landing.shape[1]), 0).astype(F32)
+    index = jnp.sum(
+        jnp.where(row == landing, index_ref[...], 0.0), axis=0, keepdims=True
+    )
+    land = hot(row == index)
     rest = arrived_ref[:, 256:384]
     main = mm_split(
         land, jnp.concatenate([arrived_ref[:, 0:128], arrived_ref[:, 128:256]], axis=0)
     )
     rest = mm_split(land, jnp.concatenate([rest[:, 0:32], rest[:, 32:64]], axis=0))
-    leaf = main.shape[0]
-    out_ref[:leaf] = main
-    out_ref[leaf:] = jnp.concatenate(
+    rest = jnp.concatenate(
         [rest[leaf // 4 * k : leaf // 4 * (k + 1)] for k in range(4)], axis=1
     )
-
-
-def cluster_kernel(arrived_ref, land_ref, forward_ref, transposed_ref):
+    for c in range(out_ref.shape[0]):
+        out_ref[c, :leaf] = main
+        out_ref[c, leaf:] = rest
+
+
+def cluster_rows(arrived_ref, recv_ref, forward_ref, transposed_ref):
+    devices, leaf = arrived_ref.shape[0], forward_ref.shape[1]
+    land = jnp.concatenate(
+        [
+            hot(recv_ref[:, CAP + g : CAP + g + 1] == iota((devices, leaf), 1))
+            for g in range(2)
+        ],
+        axis=0,
+    )
     first = jnp.transpose(arrived_ref[:, 0:128])
     second = jnp.transpose(arrived_ref[:, 128:256])
     rest = jnp.transpose(arrived_ref[:, 256:384])
@@ -267,7 +296,7 @@
         ],
         axis=1,
     )
-    joined = mm_hot(columns, land_ref[...])
+    joined = mm_hot(columns, land)
     forward_ref[...] = joined[:HALF]
     transposed_ref[...] = joined[HALF:]
 
@@ -349,7 +378,16 @@
     return mm_full(split3(lower), split3(jnp.concatenate(solved, axis=0)))
 
 
-def leaf_kernel(spread_ref, order_ref, interp_ref):
+def leaf_kernel(
+    spread_ref,
+    order_ref,
+    arrived_ref,
+    recv_ref,
+    interp_ref,
+    forward_ref,
+    transposed_ref,
+):
+    cluster_rows(arrived_ref, recv_ref, forward_ref, transposed_ref)
     columns = spread_ref.shape[0]
     leaf, rank = interp_ref.shape
     quarter = leaf // 4
@@ -403,11 +441,12 @@
     def exchange(x):
         return lax.all_to_all(x, "rows", split_axis=0, concat_axis=0, tiled=True)
 
-    message, front_order = call(
+    positions = cluster_pos.reshape(1, local_rows)
+    message = call(
         request_kernel,
-        [shape((devices, 128), jnp.int32), shape((devices, 128), jnp.int32)],
+        shape((devices, 128), jnp.int32),
         pltpu.with_memory_space_constraint(targets, pltpu.HBM),
-        pltpu.with_memory_space_constraint(cluster_pos.reshape(1, local_rows), pltpu.HBM),
+        pltpu.with_memory_space_constraint(positions, pltpu.HBM),
         hbm=(0, 1),
         scratch=[
             pltpu.VMEM((1, block), jnp.int32),
@@ -416,19 +455,27 @@
         ],
     )
     received = exchange(message)
-    slots, member, rank, masked = call(
-        tile_prep_kernel,
+    prepared = call(
+        prep_kernel,
         [
             shape((CAP * devices, block), BF16),
             shape((devices, block), BF16),
             shape((8, block), F32),
             shape((block, block), BF16),
+            shape((devices, 128), jnp.int32),
+            shape((local_rows, local_rows), BF16),
+            shape((local_rows, local_rows), F32),
+            shape((128, 1024), BF16),
         ],
         targets,
         pattern[0],
         updates[0],
+        positions,
+        pivots,
         smem=(1,),
     )
+    received, *prepared = lax.optimization_barrier((received, *prepared))
+    slots, member, rank, masked, rows, order, index, scale = prepared
     reply = call(
         reply_kernel,
         shape((devices, 8, 128), BF16),
@@ -438,19 +485,6 @@
         scratch=[pltpu.VMEM((devices * 8, 128), F32)],
     )
     fetched = exchange(reply)
-    move, land, leaf_land, scale, order = call(
-        front_prep_kernel,
-        [
-            shape((2 * devices, CAP * devices), BF16),
-            shape((2 * devices, local_rows), BF16),
-            shape((local_rows, 2 * devices), BF16),
-            shape((128, 1024), BF16),
-            shape((local_rows, local_rows), BF16),
-        ],
-        received,
-        front_order,
-        pivots,
-    )
     outgoing = call(
         tile_kernel,
         shape((devices, 8, 128), jnp.int16),
@@ -466,30 +500,32 @@
         front_kernel,
         shape((devices, 384), F32),
         incoming,
-        move,
+        received,
+        rows,
         scale,
         scratch=[pltpu.VMEM((devices * 8, 128), F32)],
     )
     arrived = exchange(moved)
+    columns = lax.axis_size("cols")
     packed = call(
-        pack_kernel, shape((local_rows * 5 // 4, 128), F32), arrived, leaf_land
-    )
-    columns = lax.axis_size("cols")
-    spread = lax.all_to_all(
-        jnp.broadcast_to(packed[None], (columns,) + packed.shape),
-        "cols",
-        split_axis=0,
-        concat_axis=0,
-        tiled=True,
-    )
-    forward, transposed = call(
-        cluster_kernel,
-        [shape((width, local_rows), F32), shape((width, local_rows), F32)],
+        pack_kernel,
+        shape((columns, local_rows * 5 // 4, 128), F32),
         arrived,
-        land,
-    )
-    interp = call(
-        leaf_kernel, shape((local_rows, pivots.shape[1]), F32), spread, order
+        received,
+        index,
+    )
+    spread = lax.all_to_all(packed, "cols", split_axis=0, concat_axis=0, tiled=True)
+    interp, forward, transposed = call(
+        leaf_kernel,
+        [
+            shape((local_rows, pivots.shape[1]), F32),
+            shape((width, local_rows), F32),
+            shape((width, local_rows), F32),
+        ],
+        spread,
+        order,
+        arrived,
+        received,
     )
     return forward.T, transposed.T, interp
 

time: 120 us -> 117 us (0.975)
  waiting for transfers between devices: 37.1 us -> 8.37 us
  blocking collectives: 48.8 us -> 73.5 us
  starting transfers between devices: 15.4 us -> 18.4 us
  Pallas kernels: 15.3 us -> 13.3 us
    all_to_all x2 -> x1, waiting for transfers between devices: 27.7 us -> 8.37 us  [exchange(): return lax.all_to_all(x, 'rows', split_axis=0, concat_axis=0, tiled=True)]
    all_to_all x0 -> x1, blocking collectives: none -> 13.8 us  [per_device(): lax.all_to_all(packed, 'cols', split_axis=0, concat_axis=0, tiled=True)]
    all_to_all x2 -> x3, blocking collectives: 48.8 us -> 59.7 us  [exchange(): return lax.all_to_all(x, 'rows', split_axis=0, concat_axis=0, tiled=True)]
    all_to_all x1 -> x0, waiting for transfers between devices: 9.34 us -> none  [per_device(): lax.all_to_all(jnp.broadcast_to(packed[None], (columns,) + packed.shape),...]
    all_to_all x2 -> x1, starting transfers between devices: 11.4 us -> 18.4 us  [exchange(): return lax.all_to_all(x, 'rows', split_axis=0, concat_axis=0, tiled=True)]
    all_to_all x1 -> x0, starting transfers between devices: 4.01 us -> none  [per_device(): lax.all_to_all(jnp.broadcast_to(packed[None], (columns,) + packed.shape),...]
    pallas_call x9 -> x7, Pallas kernels: 15.3 us -> 13.3 us  [call(): pl.pallas_call(kernel, out_shape=outs, in_specs=spec, out_specs=jax.tree....]
  transfers between devices with their start and end apart: 3 -> 1, of which waited for: 3 -> 1; matrix products, arithmetic and copies ran while one was open for 0% -> 0% of each run, Pallas kernels for 2% -> 1%
where the time goes in v4:
time: 117 us; the launch traced here: 116 us
  blocking collectives  73.5 us (63%)
  starting transfers between devices  18.4 us (16%)
  Pallas kernels  13.3 us (11%)
  waiting for transfers between devices  8.37 us (7%)
  local copies, waits for them, and re-layouts  1.94 us (2%)
    all_to_all x3, blocking collectives, exchange(): return lax.all_to_all(x, 'rows', split_axis=0, concat_axis=0, tiled=True)  59.7 us
    all_to_all x1, starting transfers between devices, exchange(): return lax.all_to_all(x, 'rows', split_axis=0, concat_axis=0, tiled=True)  18.4 us
    all_to_all x1, blocking collectives, per_device(): lax.all_to_all(packed, 'cols', split_axis=0, concat_axis=0, tiled=True)  13.8 us
    pallas_call x7, Pallas kernels, call(): pl.pallas_call(kernel, out_shape=outs, in_specs=spec, out_specs=jax.tree....  13.3 us
    all_to_all x1, waiting for transfers between devices, exchange(): return lax.all_to_all(x, 'rows', split_axis=0, concat_axis=0, tiled=True)  8.37 us
  transfers between devices with their start and end apart: 1, of which 1 were waited for; matrix products, arithmetic and copies ran while one was open for 0% of the time, Pallas kernels for 1%

profile of v4, /device:TPU:1, one launch (start us, length us, event | category | flops | bytes accessed | tf_op | source)
XLA Modules:
  0.0 116.3 jit_solution(2904807838505343021)
XLA Ops:
  0.6 1.8 %shard_map.94 = s32[128,128]{1,0:T(8,128)} custom-call(s32[1,512]{1,0:T(1,128)} %targets_ref.1, s32[1,256]{1,0:T(1,128)} %bitcast.25), custom_call_target="tpu_custom_call" | custom-call | flops 1000000 | bytes 1000000 | tf_op jit(solution)/shard_map/pallas_call | solution.py:422
  2.5 0.0 copy-start.5
  2.5 18.4 %all-to-all-start = ((s32[128,1,128]{2,1,0:T(1,128)}), s32[128,1,128]{2,1,0:T(1,128)S(1)}, u32[]{:S(2)}, u32[]{:S(2)}) async-start(s32[128,1,128]{2,1,0:T(1,128)} %bitcast.2), calls=%async_computation | async-start | bytes 131072 | tf_op jit(solution)/shard_map/all_to_all | solution.py:442
  20.9 0.0 copy-start.3
  20.9 0.0 copy-start.4
  21.0 0.0 copy-start.6
  21.0 0.0 copy-done.5
  21.0 0.6 copy-done.3
  21.6 0.0 copy-done.4
  21.6 0.0 copy-done.6
  21.6 1.0 copy-done
  22.7 1.2 %shard_map.95 = (bf16[768,512]{1,0:T(8,128)(2,1)S(1)}, bf16[128,512]{1,0:T(8,128)(2,1)S(1)}, f32[8,512]{1,0:T(8,128)S(1)}, bf16[512,512]{1,0:T(8,128)(2,1)S(1)},...) custom-call(s32[1,512]{1,0:T(1,128)S(1)} %copy-done.3, ...), custom_call_target="tpu_custom_call" | custom-call | flops 1000000 | bytes 1000000 | tf_op jit(solution)/shard_map/pallas_call | solution.py:422
  23.9 8.4 %all-to-all-done = s32[128,1,128]{2,1,0:T(1,128)S(1)} async-done(((s32[128,1,128]{2,1,0:T(1,128)}), s32[128,1,128]{2,1,0:T(1,128)S(1)}, u32[]{:S(2)}, u32[]{:S(2)}) %all-to-all-start) | async-done | bytes 65568 | tf_op jit(solution)/shard_map/all_to_all | solution.py:442
  32.3 0.0 copy-done.1
  32.3 0.4 shard_map.96
  32.8 20.5 %all_to_all.38.fetched_ref = bf16[128,8,128]{2,1,0:T(8,128)(2,1)S(1)} all-to-all(bf16[128,8,128]{2,1,0:T(8,128)(2,1)S(1)} %shard_map.96), channel_id=1, replica_groups=mesh['rows'=128,'cols'=4] {'rows'}, dimensions={0} | all-to-all | bytes 524288 | tf_op jit(solution)/shard_map/all_to_all | solution.py:442
  53.2 1.3 %shard_map.97 = s16[128,8,128]{2,1,0:T(8,128)(2,1)S(1)} custom-call(bf16[128,8,128]{2,1,0:T(8,128)(2,1)S(1)} %all_to_all.38.fetched_ref, bf16[768,512]{1,0:T(8,128)(2,1)S(1)} %get-tuple-element.32.slots_ref, bf16[128,512]{1,0:T(8,128)(2,1)S(1)} %get-tuple-element.33.member_ref, f32[8,512]{1,0:T(8,128)S(1)} %get-tuple-element.34.rank_ref, ...), custom_call_target="tpu_custom_call" | custom-call | flops 1000000 | bytes 1000000 | tf_op jit(solution)/shard_map/pallas_call | solution.py:422
  54.6 20.3 %all_to_all.39.incoming_ref = s16[128,8,128]{2,1,0:T(8,128)(2,1)S(1)} all-to-all(s16[128,8,128]{2,1,0:T(8,128)(2,1)S(1)} %shard_map.97), channel_id=1, replica_groups=mesh['rows'=128,'cols'=4] {'rows'}, dimensions={0} | all-to-all | bytes 524288 | tf_op jit(solution)/shard_map/all_to_all | solution.py:442
  74.8 1.2 %shard_map.98 = f32[128,384]{1,0:T(8,128)S(1)} custom-call(s16[128,8,128]{2,1,0:T(8,128)(2,1)S(1)} %all_to_all.39.incoming_ref, s32[128,128]{1,0:T(8,128)S(1)} %bitcast.18, s32[128,128]{1,0:T(8,128)S(1)} %get-tuple-element.36.rows_ref, bf16[128,1024]{1,0:T(8,128)(2,1)S(1)} %get-tuple-element.37.scale_ref), custom_call_target="tpu_custom_call" | custom-call | flops 1000000 | bytes 1000000 | tf_op jit(solution)/shard_map/pallas_call | solution.py:422
  76.1 0.2 copy.11
  76.3 19.0 %all_to_all.40 = f32[128,1,384]{2,1,0:T(1,128)S(1)} all-to-all(f32[128,1,384]{2,1,0:T(1,128)S(1)} %copy.11), channel_id=1, replica_groups=mesh['rows'=128,'cols'=4] {'rows'}, dimensions={0} | all-to-all | bytes 393216 | tf_op jit(solution)/shard_map/all_to_all | solution.py:442
  95.3 0.5 shard_map.99
  95.8 13.8 %all_to_all.41.spread_ref = f32[4,320,128]{2,1,0:T(8,128)S(1)} all-to-all(f32[4,320,128]{2,1,0:T(8,128)S(1)} %shard_map.99), channel_id=1, replica_groups=mesh['rows'=128,'cols'=4] {'cols'}, dimensions={0} | all-to-all | bytes 1310720 | tf_op jit(solution)/shard_map/all_to_all | solution.py:517
  109.6 6.7 %shard_map.100 = (f32[256,128]{1,0:T(8,128)}, f32[80,256]{1,0:T(8,128)}, f32[80,256]{1,0:T(8,128)}) custom-call(f32[4,320,128]{2,1,0:T(8,128)S(1)} %all_to_all.41.spread_ref, bf16[256,256]{1,0:T(8,128)(2,1)S(1)} %get-tuple-element.39.order_ref, f32[128,384]{1,0:T(8,128)S(1)} %bitcast.16, s32[128,128]{1,0:T(8,128)S(1)} %bitcast.20), custom_call_target="tpu_custom_call" | custom-call | flops 1000000 | bytes 1000000 | tf_op jit(solution)/shard_map/pallas_call | solution.py:422
  (5 shorter events, 0.0 us)
Async XLA Ops:
  2.5 18.5 %copy-start.5 = (s32[1,4,4]{2,1,0:T(4,128)S(1)}, s32[1,4,4]{2,1,0:T(4,128)}, u32[]{:S(2)}) copy-start(s32[1,4,4]{2,1,0:T(4,128)} %param.10) | copy-start | bytes 196
  2.5 29.8 %all-to-all-start = ((s32[128,1,128]{2,1,0:T(1,128)}), s32[128,1,128]{2,1,0:T(1,128)S(1)}, u32[]{:S(2)}, u32[]{:S(2)}) async-start(s32[128,1,128]{2,1,0:T(1,128)} %bitcast.2), calls=%async_computation | async-start | bytes 131072 | tf_op jit(solution)/shard_map/all_to_all | solution.py:442
  20.9 0.7 copy-start.3
  20.9 0.7 copy-start.4
  21.0 0.7 copy-start.6
  21.6 1.0 copy-start
  22.7 9.6 %copy-start.1 = (bf16[256,80]{0,1:T(8,128)(2,1)S(1)}, bf16[256,80]{0,1:T(8,128)(2,1)}, u32[]{:S(2)}) copy-start(bf16[256,80]{0,1:T(8,128)(2,1)} %param.7) | copy-start | bytes 122884
  22.7 9.6 %copy-start.2 = (bf16[256,80]{0,1:T(8,128)(2,1)S(1)}, bf16[256,80]{0,1:T(8,128)(2,1)}, u32[]{:S(2)}) copy-start(bf16[256,80]{0,1:T(8,128)(2,1)} %param.8) | copy-start | bytes 122884

commit v5 on v4

--- a/solution.py
+++ b/solution.py
@@ -85,6 +85,7 @@
     order_ref,
     index_ref,
     scale_ref,
+    leaf_scale_ref,
 ):
     devices = member_ref.shape[0]
     member, rank = ranks(targets_ref[...] >> 8, devices)
@@ -132,6 +133,11 @@
         scale_ref[:, 128 * s : 128 * s + 128] = hot(
             place == CODES + 8 + 4 * (s - 6) + (lane >> 5)
         )
+    for c in range(4):
+        leaf_scale_ref[:, 128 * c : 128 * c + 128] = hot(
+            place == 32 * c + jnp.where(lane >= HALF, 1, 0)
+        )
+    leaf_scale_ref[:, 512:640] = hot(place == 32 * (lane >> 5) + 1)
 
 
 def reply_kernel(recv_ref, right_ref, left_ref, out_ref, scratch):
@@ -158,16 +164,24 @@
     return jnp.exp(code * (LOG2 / 256.0)) * (1.0 / 32600.0)
 
 
+def code_of(peak):
+    return jnp.ceil(jnp.log(jnp.maximum(peak, 1e-32)) * (256.0 / LOG2))
+
+
 def coded(x):
-    peak = jnp.maximum(jnp.max(jnp.abs(x), axis=0, keepdims=True), 1e-32)
-    code = jnp.ceil(jnp.log(peak) * (256.0 / LOG2))
+    code = code_of(jnp.max(jnp.abs(x), axis=0, keepdims=True))
     return jnp.floor(x / steps_of(code) + 0.5), code
 
 
-def mm_whole(hots, x):
+def halves(x):
     high = jnp.floor(x * (1.0 / 256.0) + 0.5)
     low = x - 256.0 * high
-    return mm(hots, high.astype(BF16), NT) * 256.0 + mm(hots, low.astype(BF16), NT)
+    return high.astype(BF16), low.astype(BF16)
+
+
+def mm_whole(hots, x, dims=NT):
+    high, low = halves(x)
+    return mm(hots, high, dims) * 256.0 + mm(hots, low, dims)
 
 
 def tile_kernel(
@@ -211,8 +225,8 @@
     )
 
 
-def front_kernel(incoming_ref, recv_ref, rows_ref, scale_ref, out_ref, scratch):
-    devices = out_ref.shape[0]
+def front_kernel(incoming_ref, recv_ref, rows_ref, scale_ref, out_ref, scratch, sent):
+    devices = recv_ref.shape[0]
     across = jnp.transpose(recv_ref[...].astype(F32)).astype(jnp.int32)
     move = jnp.concatenate(
         [
@@ -243,11 +257,38 @@
     )
     main = mm(move, main[0]) + mm(move, main[1]) + mm(move, main[2])
     rest = mm(move, rest[0]) + mm(move, rest[1]) + mm(move, rest[2])
-    out_ref[:, 0:128] = main[:devices]
-    out_ref[:, 128:256] = main[devices:]
-    out_ref[:, 256:384] = jnp.concatenate(
-        [rest[:devices], rest[devices:], jnp.zeros((devices, 64), F32)], axis=1
-    )
+    lane = iota(main.shape, 1)
+    size = jnp.abs(main)
+    peaks = [
+        jnp.max(jnp.where(lane < HALF, size, 0.0), axis=1, keepdims=True),
+        jnp.maximum(
+            jnp.max(jnp.where(lane >= HALF, size, 0.0), axis=1, keepdims=True),
+            jnp.max(jnp.abs(rest), axis=1, keepdims=True),
+        ),
+    ]
+    codes = [code_of(peak) for peak in peaks]
+    steps = [1.0 / steps_of(code) for code in codes]
+    main = jnp.floor(main * jnp.where(lane < HALF, steps[0], steps[1]) + 0.5)
+    rest = jnp.floor(rest * steps[1] + 0.5)
+    rest = jnp.concatenate(
+        [
+            rest[:devices],
+            jnp.zeros((devices, 8), F32),
+            rest[devices:],
+            jnp.zeros((devices, 56), F32),
+        ],
+        axis=1,
+    )
+    lane = iota(rest.shape, 1)
+    for g in range(2):
+        for h in range(2):
+            code = codes[h][g * devices : (g + 1) * devices]
+            rest = jnp.where(lane == 40 * g + 32 + h, code, rest)
+    sent[pl.ds(0, devices, stride=4), :] = main[:devices]
+    sent[pl.ds(1, devices, stride=4), :] = main[devices:]
+    sent[pl.ds(2, devices, stride=4), :] = rest
+    sent[pl.ds(3, devices, stride=4), :] = jnp.zeros_like(rest)
+    out_ref[...] = sent[...].astype(jnp.int32).astype(jnp.int16)
 
 
 def mm_split(hots, x):
@@ -255,8 +296,12 @@
     return mm(hots, x0) + mm(hots, x1) + mm(hots, x2)
 
 
-def pack_kernel(arrived_ref, recv_ref, index_ref, out_ref):
-    leaf = index_ref.shape[0]
+def pack_kernel(arrived_ref, recv_ref, index_ref, out_ref, plane_ref, scratch):
+    leaf, devices = index_ref.shape[0], recv_ref.shape[0]
+    scratch[...] = arrived_ref[...].astype(jnp.int32).astype(F32)
+    plane = [scratch[pl.ds(r, devices, stride=4), :] for r in range(3)]
+    for r in range(3):
+        plane_ref[r * devices : (r + 1) * devices, :] = plane[r]
     across = jnp.transpose(recv_ref[...].astype(F32))
     landing = jnp.concatenate([across[CAP : CAP + 1], across[CAP + 1 : CAP + 2]], axis=1)
     row = iota((leaf, landing.shape[1]), 0).astype(F32)
@@ -264,21 +309,26 @@
         jnp.where(row == landing, index_ref[...], 0.0), axis=0, keepdims=True
     )
     land = hot(row == index)
-    rest = arrived_ref[:, 256:384]
-    main = mm_split(
-        land, jnp.concatenate([arrived_ref[:, 0:128], arrived_ref[:, 128:256]], axis=0)
-    )
-    rest = mm_split(land, jnp.concatenate([rest[:, 0:32], rest[:, 32:64]], axis=0))
-    rest = jnp.concatenate(
-        [rest[leaf // 4 * k : leaf // 4 * (k + 1)] for k in range(4)], axis=1
-    )
+    main = mm_whole(land, jnp.concatenate(plane[:2], axis=0), NN)
+    rest = jnp.concatenate([plane[2][:, 0:40], plane[2][:, 40:80]], axis=0)
+    rest = jnp.concatenate([rest, jnp.zeros((rest.shape[0], 24), F32)], axis=1)
+    rest = mm_whole(land, rest, NN)
+    part = [rest[leaf // 4 * k : leaf // 4 * (k + 1)] for k in range(4)]
+    rows = jnp.concatenate(
+        [
+            main,
+            jnp.concatenate([x[:, 0:32] for x in part], axis=1),
+            jnp.concatenate([x[:, 32:64] for x in part], axis=1),
+        ],
+        axis=0,
+    )
+    rows = rows.astype(jnp.int32).astype(jnp.int16)
     for c in range(out_ref.shape[0]):
-        out_ref[c, :leaf] = main
-        out_ref[c, leaf:] = rest
-
-
-def cluster_rows(arrived_ref, recv_ref, forward_ref, transposed_ref):
-    devices, leaf = arrived_ref.shape[0], forward_ref.shape[1]
+        out_ref[c] = rows
+
+
+def cluster_rows(plane_ref, recv_ref, forward_ref, transposed_ref):
+    devices, leaf = recv_ref.shape[0], forward_ref.shape[1]
     land = jnp.concatenate(
         [
             hot(recv_ref[:, CAP + g : CAP + g + 1] == iota((devices, leaf), 1))
@@ -286,19 +336,20 @@
         ],
         axis=0,
     )
-    first = jnp.transpose(arrived_ref[:, 0:128])
-    second = jnp.transpose(arrived_ref[:, 128:256])
-    rest = jnp.transpose(arrived_ref[:, 256:384])
+    first, second, rest = [
+        jnp.transpose(plane_ref[r * devices : (r + 1) * devices, :]) for r in range(3)
+    ]
     columns = jnp.concatenate(
         [
-            jnp.concatenate([first, rest[0:32]], axis=0),
-            jnp.concatenate([second, rest[32:64]], axis=0),
+            jnp.concatenate([first, rest[0:40]], axis=0),
+            jnp.concatenate([second, rest[40:80]], axis=0),
         ],
         axis=1,
     )
-    joined = mm_hot(columns, land)
-    forward_ref[...] = joined[:HALF]
-    transposed_ref[...] = joined[HALF:]
+    high, low = halves(columns)
+    joined = mm(high, land) * 256.0 + mm(low, land)
+    forward_ref[...] = joined[:HALF] * steps_of(joined[160:161])
+    transposed_ref[...] = joined[HALF:160] * steps_of(joined[161:162])
 
 
 def mm_full(a, b, dims=NN):
@@ -381,27 +432,34 @@
 def leaf_kernel(
     spread_ref,
     order_ref,
-    arrived_ref,
+    leaf_scale_ref,
+    plane_ref,
     recv_ref,
     interp_ref,
     forward_ref,
     transposed_ref,
 ):
-    cluster_rows(arrived_ref, recv_ref, forward_ref, transposed_ref)
+    cluster_rows(plane_ref, recv_ref, forward_ref, transposed_ref)
     columns = spread_ref.shape[0]
     leaf, rank = interp_ref.shape
     quarter = leaf // 4
-    rest = [spread_ref[c, leaf:, :] for c in range(columns)]
-    rest = jnp.concatenate(
-        [
-            jnp.concatenate([x[:, 32 * k : 32 * k + 32] for x in rest], axis=1)
-            for k in range(4)
-        ],
-        axis=0,
-    )
-    rows = split3(
-        jnp.concatenate([spread_ref[c, :leaf, :] for c in range(columns)] + [rest], axis=1)
-    )
+    got = [spread_ref[c].astype(jnp.int32).astype(F32) for c in range(columns)]
+
+    def unpacked(first):
+        return jnp.concatenate(
+            [
+                jnp.concatenate(
+                    [x[first : first + quarter, 32 * k : 32 * k + 32] for x in got],
+                    axis=1,
+                )
+                for k in range(4)
+            ],
+            axis=0,
+        )
+
+    rows = jnp.concatenate([x[:leaf] for x in got] + [unpacked(leaf)], axis=1)
+    steps = mm_hot(steps_of(unpacked(leaf + quarter)), leaf_scale_ref[...])
+    rows = split3(rows * steps)
     pivots = [part[:rank] for part in rows]
     others = [part[rank:] for part in rows]
     eye = jnp.where(iota((rank, rank), 0) == iota((rank, rank), 1), 1.0, 0.0)
@@ -466,6 +524,7 @@
             shape((local_rows, local_rows), BF16),
             shape((local_rows, local_rows), F32),
             shape((128, 1024), BF16),
+            shape((128, 640), BF16),
         ],
         targets,
         pattern[0],
@@ -475,7 +534,7 @@
         smem=(1,),
     )
     received, *prepared = lax.optimization_barrier((received, *prepared))
-    slots, member, rank, masked, rows, order, index, scale = prepared
+    slots, member, rank, masked, rows, order, index, scale, leaf_scale = prepared
     reply = call(
         reply_kernel,
         shape((devices, 8, 128), BF16),
@@ -498,21 +557,28 @@
     incoming = exchange(outgoing)
     moved = call(
         front_kernel,
-        shape((devices, 384), F32),
+        shape((devices * 4, 128), jnp.int16),
         incoming,
         received,
         rows,
         scale,
-        scratch=[pltpu.VMEM((devices * 8, 128), F32)],
-    )
-    arrived = exchange(moved)
+        scratch=[
+            pltpu.VMEM((devices * 8, 128), F32),
+            pltpu.VMEM((devices * 4, 128), F32),
+        ],
+    )
+    arrived = exchange(moved.reshape(devices, 4, 128)).reshape(devices * 4, 128)
     columns = lax.axis_size("cols")
-    packed = call(
+    packed, planes = call(
         pack_kernel,
-        shape((columns, local_rows * 5 // 4, 128), F32),
+        [
+            shape((columns, local_rows * 3 // 2, 128), jnp.int16),
+            shape((3 * devices, 128), F32),
+        ],
         arrived,
         received,
         index,
+        scratch=[pltpu.VMEM((devices * 4, 128), F32)],
     )
     spread = lax.all_to_all(packed, "cols", split_axis=0, concat_axis=0, tiled=True)
     interp, forward, transposed = call(
@@ -524,7 +590,8 @@
         ],
         spread,
         order,
-        arrived,
+        leaf_scale,
+        planes,
         received,
     )
     return forward.T, transposed.T, interp

time: 117 us -> 113 us (0.966)
  blocking collectives: 73.5 us -> 69.5 us
    all_to_all x1, blocking collectives: 13.8 us -> 11 us  [per_device(): lax.all_to_all(packed, 'cols', split_axis=0, concat_axis=0, tiled=True)]
    all_to_all x3, blocking collectives: 59.7 us -> 58.4 us  [exchange(): return lax.all_to_all(x, 'rows', split_axis=0, concat_axis=0, tiled=True)]
where the time goes in v5:
time: 113 us
  blocking collectives  69.5 us (62%)
  starting transfers between devices  18.4 us (16%)
  Pallas kernels  13.9 us (12%)
  waiting for transfers between devices  8.36 us (7%)
  local copies, waits for them, and re-layouts  1.72 us (2%)
    all_to_all x3, blocking collectives, exchange(): return lax.all_to_all(x, 'rows', split_axis=0, concat_axis=0, tiled=True)  58.4 us
    all_to_all x1, starting transfers between devices, exchange(): return lax.all_to_all(x, 'rows', split_axis=0, concat_axis=0, tiled=True)  18.4 us
    pallas_call x7, Pallas kernels, call(): pl.pallas_call(kernel, out_shape=outs, in_specs=spec, out_specs=jax.tree....  13.9 us
    all_to_all x1, blocking collectives, per_device(): lax.all_to_all(packed, 'cols', split_axis=0, concat_axis=0, tiled=True)  11 us
    all_to_all x1, waiting for transfers between devices, exchange(): return lax.all_to_all(x, 'rows', split_axis=0, concat_axis=0, tiled=True)  8.36 us
  transfers between devices with their start and end apart: 1, of which 1 were waited for; matrix products, arithmetic and copies ran while one was open for 0% of the time, Pallas kernels for 1%

profile of v5, /device:TPU:1, one launch (start us, length us, event | category | flops | bytes accessed | tf_op | source)
XLA Modules:
  0.0 112.6 jit_solution(12538121995897154966)
XLA Ops:
  0.6 1.8 %shard_map.94 = s32[128,128]{1,0:T(8,128)} custom-call(s32[1,512]{1,0:T(1,128)} %targets_ref.1, s32[1,256]{1,0:T(1,128)} %bitcast.22), custom_call_target="tpu_custom_call" | custom-call | flops 1000000 | bytes 1000000 | tf_op jit(solution)/shard_map/pallas_call | solution.py:480
  2.5 0.0 copy-start.5
  2.5 18.4 %all-to-all-start = ((s32[128,1,128]{2,1,0:T(1,128)}), s32[128,1,128]{2,1,0:T(1,128)S(1)}, u32[]{:S(2)}, u32[]{:S(2)}) async-start(s32[128,1,128]{2,1,0:T(1,128)} %bitcast.2), calls=%async_computation | async-start | bytes 131072 | tf_op jit(solution)/shard_map/all_to_all | solution.py:500
  20.9 0.0 copy-start.3
  20.9 0.0 copy-start.4
  21.0 0.0 copy-start.6
  21.0 0.0 copy-done.5
  21.0 0.6 copy-done.3
  21.6 0.0 copy-done.4
  21.6 0.0 copy-done.6
  21.6 1.0 copy-done
  22.7 1.3 %shard_map.95 = (bf16[768,512]{1,0:T(8,128)(2,1)S(1)}, bf16[128,512]{1,0:T(8,128)(2,1)S(1)}, f32[8,512]{1,0:T(8,128)S(1)}, bf16[512,512]{1,0:T(8,128)(2,1)S(1)},...) custom-call(s32[1,512]{1,0:T(1,128)S(1)} %copy-done.3, ...), custom_call_target="tpu_custom_call" | custom-call | flops 1000000 | bytes 1000000 | tf_op jit(solution)/shard_map/pallas_call | solution.py:480
  23.9 8.4 %all-to-all-done = s32[128,1,128]{2,1,0:T(1,128)S(1)} async-done(((s32[128,1,128]{2,1,0:T(1,128)}), s32[128,1,128]{2,1,0:T(1,128)S(1)}, u32[]{:S(2)}, u32[]{:S(2)}) %all-to-all-start) | async-done | bytes 65568 | tf_op jit(solution)/shard_map/all_to_all | solution.py:500
  32.3 0.0 copy-done.1
  32.3 0.0 copy-done.2
  32.3 0.4 shard_map.96
  32.8 20.5 %all_to_all.32.fetched_ref = bf16[128,8,128]{2,1,0:T(8,128)(2,1)S(1)} all-to-all(bf16[128,8,128]{2,1,0:T(8,128)(2,1)S(1)} %shard_map.96), channel_id=1, replica_groups=mesh['rows'=128,'cols'=4] {'rows'}, dimensions={0} | all-to-all | bytes 524288 | tf_op jit(solution)/shard_map/all_to_all | solution.py:500
  53.2 1.4 %shard_map.97 = s16[128,8,128]{2,1,0:T(8,128)(2,1)S(1)} custom-call(bf16[128,8,128]{2,1,0:T(8,128)(2,1)S(1)} %all_to_all.32.fetched_ref, bf16[768,512]{1,0:T(8,128)(2,1)S(1)} %get-tuple-element.37.slots_ref, bf16[128,512]{1,0:T(8,128)(2,1)S(1)} %get-tuple-element.38.member_ref, f32[8,512]{1,0:T(8,128)S(1)} %get-tuple-element.39.rank_ref, ...), custom_call_target="tpu_custom_call" | custom-call | flops 1000000 | bytes 1000000 | tf_op jit(solution)/shard_map/pallas_call | solution.py:480
  54.6 20.3 %all_to_all.33.incoming_ref = s16[128,8,128]{2,1,0:T(8,128)(2,1)S(1)} all-to-all(s16[128,8,128]{2,1,0:T(8,128)(2,1)S(1)} %shard_map.97), channel_id=1, replica_groups=mesh['rows'=128,'cols'=4] {'rows'}, dimensions={0} | all-to-all | bytes 524288 | tf_op jit(solution)/shard_map/all_to_all | solution.py:500
  74.8 1.4 %shard_map.98 = s16[512,128]{1,0:T(8,128)(2,1)S(1)} custom-call(s16[128,8,128]{2,1,0:T(8,128)(2,1)S(1)} %all_to_all.33.incoming_ref, s32[128,128]{1,0:T(8,128)S(1)} %bitcast.14, s32[128,128]{1,0:T(8,128)S(1)} %get-tuple-element.41.rows_ref, bf16[128,1024]{1,0:T(8,128)(2,1)S(1)} %get-tuple-element.42.scale_ref), custom_call_target="tpu_custom_call" | custom-call | flops 1000000 | bytes 1000000 | tf_op jit(solution)/shard_map/pallas_call | solution.py:480
  76.2 17.7 %all_to_all.34 = s16[128,4,128]{2,1,0:T(4,128)(2,1)S(1)} all-to-all(s16[128,4,128]{2,1,0:T(4,128)(2,1)S(1)} %bitcast.19), channel_id=1, replica_groups=mesh['rows'=128,'cols'=4] {'rows'}, dimensions={0} | all-to-all | bytes 262144 | tf_op jit(solution)/shard_map/all_to_all | solution.py:500
  94.0 0.5 shard_map.99
  94.5 11.0 %all_to_all.35.spread_ref = s16[4,384,128]{2,1,0:T(8,128)(2,1)S(1)} all-to-all(s16[4,384,128]{2,1,0:T(8,128)(2,1)S(1)} %get-tuple-element.44), channel_id=1, replica_groups=mesh['rows'=128,'cols'=4] {'cols'}, dimensions={0} | all-to-all | bytes 786432 | tf_op jit(solution)/shard_map/all_to_all | solution.py:583
  105.5 7.2 %shard_map.100 = (f32[256,128]{1,0:T(8,128)}, f32[80,256]{1,0:T(8,128)}, f32[80,256]{1,0:T(8,128)}) custom-call(s16[4,384,128]{2,1,0:T(8,128)(2,1)S(1)} %all_to_all.35.spread_ref, bf16[256,256]{1,0:T(8,128)(2,1)S(1)} %get-tuple-element.45.order_ref, bf16[128,640]{1,0:T(8,128)(2,1)S(1)} %get-tuple-element.46.leaf_scale_ref, ...), custom_call_target="tpu_custom_call" | custom-call | flops 1000000 | bytes 1000000 | tf_op jit(solution)/shard_map/pallas_call | solution.py:480
  (3 shorter events, 0.0 us)
Async XLA Ops:
  2.5 18.5 %copy-start.5 = (s32[1,4,4]{2,1,0:T(4,128)S(1)}, s32[1,4,4]{2,1,0:T(4,128)}, u32[]{:S(2)}) copy-start(s32[1,4,4]{2,1,0:T(4,128)} %param.10) | copy-start | bytes 196
  2.5 29.8 %all-to-all-start = ((s32[128,1,128]{2,1,0:T(1,128)}), s32[128,1,128]{2,1,0:T(1,128)S(1)}, u32[]{:S(2)}, u32[]{:S(2)}) async-start(s32[128,1,128]{2,1,0:T(1,128)} %bitcast.2), calls=%async_computation | async-start | bytes 131072 | tf_op jit(solution)/shard_map/all_to_all | solution.py:500
  20.9 0.7 copy-start.3
  20.9 0.7 copy-start.4
  21.0 0.7 copy-start.6
  21.6 1.0 copy-start
  22.7 9.6 %copy-start.1 = (bf16[256,80]{0,1:T(8,128)(2,1)S(1)}, bf16[256,80]{0,1:T(8,128)(2,1)}, u32[]{:S(2)}) copy-start(bf16[256,80]{0,1:T(8,128)(2,1)} %param.7) | copy-start | bytes 122884
  22.7 9.6 %copy-start.2 = (bf16[256,80]{0,1:T(8,128)(2,1)S(1)}, bf16[256,80]{0,1:T(8,128)(2,1)}, u32[]{:S(2)}) copy-start(bf16[256,80]{0,1:T(8,128)(2,1)} %param.8) | copy-start | bytes 122884

commit v6 on v5

--- a/solution.py
+++ b/solution.py
@@ -180,8 +180,9 @@
 
 
 def mm_whole(hots, x, dims=NT):
-    high, low = halves(x)
-    return mm(hots, high, dims) * 256.0 + mm(hots, low, dims)
+    both = mm(hots, jnp.concatenate(halves(x), axis=0 if dims == NT else 1), dims)
+    n = both.shape[1] // 2
+    return both[:, :n] * 256.0 + both[:, n:]
 
 
 def tile_kernel(
@@ -248,15 +249,14 @@
     codes = jnp.where(iota(plane[7].shape, 1) >= CODES, plane[7], 0.0)
     scales = mm_hot(steps_of(codes), scale_ref[...])
     plane = [plane[s] * scales[:, 128 * s : 128 * s + 128] for s in range(8)]
-    main = split3(jnp.concatenate(plane[:CAP], axis=0))
-    rest = split3(
-        jnp.concatenate(
-            [plane[6 + s // 4][:, 32 * (s % 4) : 32 * (s % 4) + 32] for s in range(CAP)],
-            axis=0,
-        )
-    )
-    main = mm(move, main[0]) + mm(move, main[1]) + mm(move, main[2])
-    rest = mm(move, rest[0]) + mm(move, rest[1]) + mm(move, rest[2])
+    rest = jnp.concatenate(
+        [plane[6 + s // 4][:, 32 * (s % 4) : 32 * (s % 4) + 32] for s in range(CAP)],
+        axis=0,
+    )
+    moved = mm_split(
+        move, jnp.concatenate([jnp.concatenate(plane[:CAP], axis=0), rest], axis=1)
+    )
+    main, rest = moved[:, :128], moved[:, 128:]
     lane = iota(main.shape, 1)
     size = jnp.abs(main)
     peaks = [
@@ -309,10 +309,12 @@
         jnp.where(row == landing, index_ref[...], 0.0), axis=0, keepdims=True
     )
     land = hot(row == index)
-    main = mm_whole(land, jnp.concatenate(plane[:2], axis=0), NN)
     rest = jnp.concatenate([plane[2][:, 0:40], plane[2][:, 40:80]], axis=0)
-    rest = jnp.concatenate([rest, jnp.zeros((rest.shape[0], 24), F32)], axis=1)
-    rest = mm_whole(land, rest, NN)
+    rest = jnp.concatenate([rest, jnp.zeros((rest.shape[0], 88), F32)], axis=1)
+    rows = mm_whole(
+        land, jnp.concatenate([jnp.concatenate(plane[:2], axis=0), rest], axis=1), NN
+    )
+    main, rest = rows[:, :128], rows[:, 128:]
     part = [rest[leaf // 4 * k : leaf // 4 * (k + 1)] for k in range(4)]
     rows = jnp.concatenate(
         [
@@ -357,6 +359,16 @@
     b0, b1, b2 = b
     small = mm(a2, b0, dims) + mm(a1, b1, dims) + mm(a0, b2, dims)
     return (small + (mm(a1, b0, dims) + mm(a0, b1, dims))) + mm(a0, b0, dims)
+
+
+def mm_pair(a, b):
+    a0, a1, a2 = a
+    b0, b1, b2 = b
+    n = b0.shape[0]
+    pair = jnp.concatenate([b0, b1], axis=0)
+    first, second = mm(a0, pair, NT), mm(a1, pair, NT)
+    small = mm(a2, b0, NT) + mm(a0, b2, NT) + second[:, n:]
+    return (small + (second[:, :n] + first[:, n:])) + first[:, :n]
 
 
 def mm_hot(a, b):
@@ -396,6 +408,7 @@
     shape = a[0].shape
     sub, lane = iota(shape, 0), iota(shape, 1)
     lower, solved = [], []
+    zero = jnp.zeros(shape, F32)
 
     def spread(x):
         return jnp.broadcast_to(x, shape)
@@ -420,11 +433,23 @@
             picked = jnp.where(sub == q, new[q], picked)
         lower.append(jnp.where(lane < k + b, left, 0.0))
         solved.append(jnp.where(lane < k + b, picked, 0.0))
-        for i in range(g + 1, n // b):
-            terms = [spread(a[i][:, k + q : k + q + 1]) * new[q] for q in range(b)]
+        if g + 1 < n // b:
+            terms = [spread(a[g + 1][:, k + q : k + q + 1]) * new[q] for q in range(b)]
             while len(terms) > 1:
                 terms = [terms[t] + terms[t + 1] for t in range(0, len(terms), 2)]
-            a[i] = jnp.where(inside, 0.0, a[i]) - terms[0]
+            a[g + 1] = jnp.where(inside, 0.0, a[g + 1]) - terms[0]
+        if g + 2 < n // b:
+            x0, x1, x2 = split3(jnp.concatenate(a[g + 2 :], axis=0))
+            y0, y1, y2 = split3(
+                jnp.concatenate([picked if i == g else zero for i in range(n // b)], axis=0)
+            )
+            change = mm(
+                jnp.concatenate([x0, x0, x0, x1, x1, x2], axis=1),
+                jnp.concatenate([y0, y1, y2, y0, y1, y0], axis=0),
+            )
+            for i in range(g + 2, n // b):
+                first = b * (i - g - 2)
+                a[i] = jnp.where(inside, 0.0, a[i]) - change[first : first + b]
     lower = jnp.transpose(jnp.concatenate(lower, axis=0))
     return mm_full(split3(lower), split3(jnp.concatenate(solved, axis=0)))
 
@@ -463,8 +488,8 @@
     pivots = [part[:rank] for part in rows]
     others = [part[rank:] for part in rows]
     eye = jnp.where(iota((rank, rank), 0) == iota((rank, rank), 1), 1.0, 0.0)
-    gram = mm_full(pivots, pivots, NT) * (1.0 / (2.0 * K)) + eye
-    cross = mm_full(others, pivots, NT) * (1.0 / (2.0 * K))
+    gram = mm_pair(pivots, pivots) * (1.0 / (2.0 * K)) + eye
+    cross = mm_pair(others, pivots) * (1.0 / (2.0 * K))
     chosen = order_ref[:, :rank].astype(F32)
     cross = split3(mm_split(order_ref[:, rank:], cross) - chosen)
     interp_ref[...] = chosen + mm_full(cross, split3(inverse(gram)))

time: 113 us -> 112 us (level)
  Pallas kernels: 13.9 us -> 12.5 us
    pallas_call x7, Pallas kernels: 13.9 us -> 12.5 us  [call(): pl.pallas_call(kernel, out_shape=outs, in_specs=spec, out_specs=jax.tree....]
where the time goes in v6:
time: 112 us; the launch traced here: 111 us
  blocking collectives  69.4 us (62%)
  starting transfers between devices  18.4 us (16%)
  Pallas kernels  12.5 us (11%)
  waiting for transfers between devices  8.36 us (7%)
  local copies, waits for them, and re-layouts  1.72 us (2%)
    all_to_all x3, blocking collectives, exchange(): return lax.all_to_all(x, 'rows', split_axis=0, concat_axis=0, tiled=True)  58.4 us
    all_to_all x1, starting transfers between devices, exchange(): return lax.all_to_all(x, 'rows', split_axis=0, concat_axis=0, tiled=True)  18.4 us
    pallas_call x7, Pallas kernels, call(): pl.pallas_call(kernel, out_shape=outs, in_specs=spec, out_specs=jax.tree....  12.5 us
    all_to_all x1, blocking collectives, per_device(): lax.all_to_all(packed, 'cols', split_axis=0, concat_axis=0, tiled=True)  11 us
    all_to_all x1, waiting for transfers between devices, exchange(): return lax.all_to_all(x, 'rows', split_axis=0, concat_axis=0, tiled=True)  8.36 us
  transfers between devices with their start and end apart: 1, of which 1 were waited for; matrix products, arithmetic and copies ran while one was open for 0% of the time, Pallas kernels for 1%

profile of v6, /device:TPU:1, one launch (start us, length us, event | category | flops | bytes accessed | tf_op | source)
XLA Modules:
  0.0 111.2 jit_solution(12979275968604082716)
XLA Ops:
  0.6 1.8 %shard_map.94 = s32[128,128]{1,0:T(8,128)} custom-call(s32[1,512]{1,0:T(1,128)} %targets_ref.1, s32[1,256]{1,0:T(1,128)} %bitcast.22), custom_call_target="tpu_custom_call" | custom-call | flops 1000000 | bytes 1000000 | tf_op jit(solution)/shard_map/pallas_call | solution.py:505
  2.5 0.0 copy-start.5
  2.5 18.4 %all-to-all-start = ((s32[128,1,128]{2,1,0:T(1,128)}), s32[128,1,128]{2,1,0:T(1,128)S(1)}, u32[]{:S(2)}, u32[]{:S(2)}) async-start(s32[128,1,128]{2,1,0:T(1,128)} %bitcast.2), calls=%async_computation | async-start | bytes 131072 | tf_op jit(solution)/shard_map/all_to_all | solution.py:525
  20.9 0.0 copy-start.3
  20.9 0.0 copy-start.4
  21.0 0.0 copy-start.6
  21.0 0.0 copy-done.5
  21.0 0.6 copy-done.3
  21.6 0.0 copy-done.4
  21.6 0.0 copy-done.6
  21.6 1.0 copy-done
  22.7 1.3 %shard_map.95 = (bf16[768,512]{1,0:T(8,128)(2,1)S(1)}, bf16[128,512]{1,0:T(8,128)(2,1)S(1)}, f32[8,512]{1,0:T(8,128)S(1)}, bf16[512,512]{1,0:T(8,128)(2,1)S(1)},...) custom-call(s32[1,512]{1,0:T(1,128)S(1)} %copy-done.3, ...), custom_call_target="tpu_custom_call" | custom-call | flops 1000000 | bytes 1000000 | tf_op jit(solution)/shard_map/pallas_call | solution.py:505
  23.9 8.4 %all-to-all-done = s32[128,1,128]{2,1,0:T(1,128)S(1)} async-done(((s32[128,1,128]{2,1,0:T(1,128)}), s32[128,1,128]{2,1,0:T(1,128)S(1)}, u32[]{:S(2)}, u32[]{:S(2)}) %all-to-all-start) | async-done | bytes 65568 | tf_op jit(solution)/shard_map/all_to_all | solution.py:525
  32.3 0.0 copy-done.1
  32.3 0.0 copy-done.2
  32.3 0.4 shard_map.96
  32.8 20.5 %all_to_all.32.fetched_ref = bf16[128,8,128]{2,1,0:T(8,128)(2,1)S(1)} all-to-all(bf16[128,8,128]{2,1,0:T(8,128)(2,1)S(1)} %shard_map.96), channel_id=1, replica_groups=mesh['rows'=128,'cols'=4] {'rows'}, dimensions={0} | all-to-all | bytes 524288 | tf_op jit(solution)/shard_map/all_to_all | solution.py:525
  53.2 1.2 %shard_map.97 = s16[128,8,128]{2,1,0:T(8,128)(2,1)S(1)} custom-call(bf16[128,8,128]{2,1,0:T(8,128)(2,1)S(1)} %all_to_all.32.fetched_ref, bf16[768,512]{1,0:T(8,128)(2,1)S(1)} %get-tuple-element.37.slots_ref, bf16[128,512]{1,0:T(8,128)(2,1)S(1)} %get-tuple-element.38.member_ref, f32[8,512]{1,0:T(8,128)S(1)} %get-tuple-element.39.rank_ref, ...), custom_call_target="tpu_custom_call" | custom-call | flops 1000000 | bytes 1000000 | tf_op jit(solution)/shard_map/pallas_call | solution.py:505
  54.4 20.3 %all_to_all.33.incoming_ref = s16[128,8,128]{2,1,0:T(8,128)(2,1)S(1)} all-to-all(s16[128,8,128]{2,1,0:T(8,128)(2,1)S(1)} %shard_map.97), channel_id=1, replica_groups=mesh['rows'=128,'cols'=4] {'rows'}, dimensions={0} | all-to-all | bytes 524288 | tf_op jit(solution)/shard_map/all_to_all | solution.py:525
  74.7 1.2 %shard_map.98 = s16[512,128]{1,0:T(8,128)(2,1)S(1)} custom-call(s16[128,8,128]{2,1,0:T(8,128)(2,1)S(1)} %all_to_all.33.incoming_ref, s32[128,128]{1,0:T(8,128)S(1)} %bitcast.14, s32[128,128]{1,0:T(8,128)S(1)} %get-tuple-element.41.rows_ref, bf16[128,1024]{1,0:T(8,128)(2,1)S(1)} %get-tuple-element.42.scale_ref), custom_call_target="tpu_custom_call" | custom-call | flops 1000000 | bytes 1000000 | tf_op jit(solution)/shard_map/pallas_call | solution.py:505
  75.9 17.7 %all_to_all.34 = s16[128,4,128]{2,1,0:T(4,128)(2,1)S(1)} all-to-all(s16[128,4,128]{2,1,0:T(4,128)(2,1)S(1)} %bitcast.19), channel_id=1, replica_groups=mesh['rows'=128,'cols'=4] {'rows'}, dimensions={0} | all-to-all | bytes 262144 | tf_op jit(solution)/shard_map/all_to_all | solution.py:525
  93.7 0.4 shard_map.99
  94.1 11.0 %all_to_all.35.spread_ref = s16[4,384,128]{2,1,0:T(8,128)(2,1)S(1)} all-to-all(s16[4,384,128]{2,1,0:T(8,128)(2,1)S(1)} %get-tuple-element.44), channel_id=1, replica_groups=mesh['rows'=128,'cols'=4] {'cols'}, dimensions={0} | all-to-all | bytes 786432 | tf_op jit(solution)/shard_map/all_to_all | solution.py:608
  105.1 6.2 %shard_map.100 = (f32[256,128]{1,0:T(8,128)}, f32[80,256]{1,0:T(8,128)}, f32[80,256]{1,0:T(8,128)}) custom-call(s16[4,384,128]{2,1,0:T(8,128)(2,1)S(1)} %all_to_all.35.spread_ref, bf16[256,256]{1,0:T(8,128)(2,1)S(1)} %get-tuple-element.45.order_ref, bf16[128,640]{1,0:T(8,128)(2,1)S(1)} %get-tuple-element.46.leaf_scale_ref, ...), custom_call_target="tpu_custom_call" | custom-call | flops 1000000 | bytes 1000000 | tf_op jit(solution)/shard_map/pallas_call | solution.py:505
  (3 shorter events, 0.0 us)
Async XLA Ops:
  2.5 18.5 %copy-start.5 = (s32[1,4,4]{2,1,0:T(4,128)S(1)}, s32[1,4,4]{2,1,0:T(4,128)}, u32[]{:S(2)}) copy-start(s32[1,4,4]{2,1,0:T(4,128)} %param.10) | copy-start | bytes 196
  2.5 29.8 %all-to-all-start = ((s32[128,1,128]{2,1,0:T(1,128)}), s32[128,1,128]{2,1,0:T(1,128)S(1)}, u32[]{:S(2)}, u32[]{:S(2)}) async-start(s32[128,1,128]{2,1,0:T(1,128)} %bitcast.2), calls=%async_computation | async-start | bytes 131072 | tf_op jit(solution)/shard_map/all_to_all | solution.py:525
  20.9 0.7 copy-start.3
  20.9 0.7 copy-start.4
  21.0 0.7 copy-start.6
  21.6 1.0 copy-start
  22.7 9.6 %copy-start.1 = (bf16[256,80]{0,1:T(8,128)(2,1)S(1)}, bf16[256,80]{0,1:T(8,128)(2,1)}, u32[]{:S(2)}) copy-start(bf16[256,80]{0,1:T(8,128)(2,1)} %param.7) | copy-start | bytes 122884
  22.7 9.6 %copy-start.2 = (bf16[256,80]{0,1:T(8,128)(2,1)S(1)}, bf16[256,80]{0,1:T(8,128)(2,1)}, u32[]{:S(2)}) copy-start(bf16[256,80]{0,1:T(8,128)(2,1)} %param.8) | copy-start | bytes 122884

commit v7 on v6

--- a/solution.py
+++ b/solution.py
@@ -135,9 +135,9 @@
         )
     for c in range(4):
         leaf_scale_ref[:, 128 * c : 128 * c + 128] = hot(
-            place == 32 * c + jnp.where(lane >= HALF, 1, 0)
+            place == 8 * c + jnp.where(lane >= HALF, 1, 0)
         )
-    leaf_scale_ref[:, 512:640] = hot(place == 32 * (lane >> 5) + 1)
+    leaf_scale_ref[:, 512:640] = hot(place == 8 * (lane >> 5) + 1)
 
 
 def reply_kernel(recv_ref, right_ref, left_ref, out_ref, scratch):
@@ -320,7 +320,9 @@
         [
             main,
             jnp.concatenate([x[:, 0:32] for x in part], axis=1),
-            jnp.concatenate([x[:, 32:64] for x in part], axis=1),
+            jnp.concatenate(
+                [rest[16 * k : 16 * k + 16, 32:40] for k in range(leaf // 16)], axis=1
+            ),
         ],
         axis=0,
     )
@@ -357,8 +359,11 @@
 def mm_full(a, b, dims=NN):
     a0, a1, a2 = a
     b0, b1, b2 = b
-    small = mm(a2, b0, dims) + mm(a1, b1, dims) + mm(a0, b2, dims)
-    return (small + (mm(a1, b0, dims) + mm(a0, b1, dims))) + mm(a0, b0, dims)
+    return mm(
+        jnp.concatenate([a2, a1, a0, a1, a0, a0], axis=1),
+        jnp.concatenate([b0, b1, b2, b0, b1, b0], axis=1 if dims == NT else 0),
+        dims,
+    )
 
 
 def mm_pair(a, b):
@@ -464,32 +469,34 @@
     forward_ref,
     transposed_ref,
 ):
-    cluster_rows(plane_ref, recv_ref, forward_ref, transposed_ref)
     columns = spread_ref.shape[0]
     leaf, rank = interp_ref.shape
     quarter = leaf // 4
     got = [spread_ref[c].astype(jnp.int32).astype(F32) for c in range(columns)]
 
-    def unpacked(first):
+    def unpacked(first, count, width):
         return jnp.concatenate(
             [
                 jnp.concatenate(
-                    [x[first : first + quarter, 32 * k : 32 * k + 32] for x in got],
+                    [x[first : first + count, width * k : width * k + width] for x in got],
                     axis=1,
                 )
-                for k in range(4)
+                for k in range(leaf // count)
             ],
             axis=0,
         )
 
-    rows = jnp.concatenate([x[:leaf] for x in got] + [unpacked(leaf)], axis=1)
-    steps = mm_hot(steps_of(unpacked(leaf + quarter)), leaf_scale_ref[...])
+    rest = unpacked(leaf, quarter, 32)
+    rows = jnp.concatenate([x[:leaf] for x in got] + [rest], axis=1)
+    codes = unpacked(leaf + quarter, 16, 8)
+    steps = mm_hot(steps_of(codes), leaf_scale_ref[: codes.shape[1], :])
     rows = split3(rows * steps)
     pivots = [part[:rank] for part in rows]
     others = [part[rank:] for part in rows]
     eye = jnp.where(iota((rank, rank), 0) == iota((rank, rank), 1), 1.0, 0.0)
     gram = mm_pair(pivots, pivots) * (1.0 / (2.0 * K)) + eye
     cross = mm_pair(others, pivots) * (1.0 / (2.0 * K))
+    cluster_rows(plane_ref, recv_ref, forward_ref, transposed_ref)
     chosen = order_ref[:, :rank].astype(F32)
     cross = split3(mm_split(order_ref[:, rank:], cross) - chosen)
     interp_ref[...] = chosen + mm_full(cross, split3(inverse(gram)))
@@ -597,7 +604,7 @@
     packed, planes = call(
         pack_kernel,
         [
-            shape((columns, local_rows * 3 // 2, 128), jnp.int16),
+            shape((columns, local_rows * 5 // 4 + 16, 128), jnp.int16),
             shape((3 * devices, 128), F32),
         ],
         arrived,

time: 112 us -> 111 us (level)
  no operation moved by 1% of the time
where the time goes in v7:
time: 111 us
  blocking collectives  69.2 us (62%)
  starting transfers between devices  18.4 us (17%)
  Pallas kernels  12.4 us (11%)
  waiting for transfers between devices  8.37 us (8%)
  local copies, waits for them, and re-layouts  1.72 us (2%)
    all_to_all x3, blocking collectives, exchange(): return lax.all_to_all(x, 'rows', split_axis=0, concat_axis=0, tiled=True)  58.4 us
    all_to_all x1, starting transfers between devices, exchange(): return lax.all_to_all(x, 'rows', split_axis=0, concat_axis=0, tiled=True)  18.4 us
    pallas_call x7, Pallas kernels, call(): pl.pallas_call(kernel, out_shape=outs, in_specs=spec, out_specs=jax.tree....  12.4 us
    all_to_all x1, blocking collectives, per_device(): lax.all_to_all(packed, 'cols', split_axis=0, concat_axis=0, tiled=True)  10.8 us
    all_to_all x1, waiting for transfers between devices, exchange(): return lax.all_to_all(x, 'rows', split_axis=0, concat_axis=0, tiled=True)  8.37 us
  transfers between devices with their start and end apart: 1, of which 1 were waited for; matrix products, arithmetic and copies ran while one was open for 0% of the time, Pallas kernels for 1%

profile of v7, /device:TPU:1, one launch (start us, length us, event | category | flops | bytes accessed | tf_op | source)
XLA Modules:
  0.0 110.8 jit_solution(17967877130667189897)
XLA Ops:
  0.6 1.8 %shard_map.94 = s32[128,128]{1,0:T(8,128)} custom-call(s32[1,512]{1,0:T(1,128)} %targets_ref.1, s32[1,256]{1,0:T(1,128)} %bitcast.22), custom_call_target="tpu_custom_call" | custom-call | flops 1000000 | bytes 1000000 | tf_op jit(solution)/shard_map/pallas_call | solution.py:512
  2.5 0.0 copy-start.5
  2.5 18.4 %all-to-all-start = ((s32[128,1,128]{2,1,0:T(1,128)}), s32[128,1,128]{2,1,0:T(1,128)S(1)}, u32[]{:S(2)}, u32[]{:S(2)}) async-start(s32[128,1,128]{2,1,0:T(1,128)} %bitcast.2), calls=%async_computation | async-start | bytes 131072 | tf_op jit(solution)/shard_map/all_to_all | solution.py:532
  20.9 0.0 copy-start.3
  20.9 0.0 copy-start.4
  21.0 0.0 copy-start.6
  21.0 0.0 copy-done.5
  21.0 0.6 copy-done.3
  21.6 0.0 copy-done.4
  21.6 0.0 copy-done.6
  21.6 1.0 copy-done
  22.7 1.3 %shard_map.95 = (bf16[768,512]{1,0:T(8,128)(2,1)S(1)}, bf16[128,512]{1,0:T(8,128)(2,1)S(1)}, f32[8,512]{1,0:T(8,128)S(1)}, bf16[512,512]{1,0:T(8,128)(2,1)S(1)},...) custom-call(s32[1,512]{1,0:T(1,128)S(1)} %copy-done.3, ...), custom_call_target="tpu_custom_call" | custom-call | flops 1000000 | bytes 1000000 | tf_op jit(solution)/shard_map/pallas_call | solution.py:512
  23.9 8.4 %all-to-all-done = s32[128,1,128]{2,1,0:T(1,128)S(1)} async-done(((s32[128,1,128]{2,1,0:T(1,128)}), s32[128,1,128]{2,1,0:T(1,128)S(1)}, u32[]{:S(2)}, u32[]{:S(2)}) %all-to-all-start) | async-done | bytes 65568 | tf_op jit(solution)/shard_map/all_to_all | solution.py:532
  32.3 0.0 copy-done.1
  32.3 0.0 copy-done.2
  32.3 0.4 shard_map.96
  32.8 20.5 %all_to_all.32.fetched_ref = bf16[128,8,128]{2,1,0:T(8,128)(2,1)S(1)} all-to-all(bf16[128,8,128]{2,1,0:T(8,128)(2,1)S(1)} %shard_map.96), channel_id=1, replica_groups=mesh['rows'=128,'cols'=4] {'rows'}, dimensions={0} | all-to-all | bytes 524288 | tf_op jit(solution)/shard_map/all_to_all | solution.py:532
  53.2 1.2 %shard_map.97 = s16[128,8,128]{2,1,0:T(8,128)(2,1)S(1)} custom-call(bf16[128,8,128]{2,1,0:T(8,128)(2,1)S(1)} %all_to_all.32.fetched_ref, bf16[768,512]{1,0:T(8,128)(2,1)S(1)} %get-tuple-element.37.slots_ref, bf16[128,512]{1,0:T(8,128)(2,1)S(1)} %get-tuple-element.38.member_ref, f32[8,512]{1,0:T(8,128)S(1)} %get-tuple-element.39.rank_ref, ...), custom_call_target="tpu_custom_call" | custom-call | flops 1000000 | bytes 1000000 | tf_op jit(solution)/shard_map/pallas_call | solution.py:512
  54.4 20.3 %all_to_all.33.incoming_ref = s16[128,8,128]{2,1,0:T(8,128)(2,1)S(1)} all-to-all(s16[128,8,128]{2,1,0:T(8,128)(2,1)S(1)} %shard_map.97), channel_id=1, replica_groups=mesh['rows'=128,'cols'=4] {'rows'}, dimensions={0} | all-to-all | bytes 524288 | tf_op jit(solution)/shard_map/all_to_all | solution.py:532
  74.7 1.2 %shard_map.98 = s16[512,128]{1,0:T(8,128)(2,1)S(1)} custom-call(s16[128,8,128]{2,1,0:T(8,128)(2,1)S(1)} %all_to_all.33.incoming_ref, s32[128,128]{1,0:T(8,128)S(1)} %bitcast.14, s32[128,128]{1,0:T(8,128)S(1)} %get-tuple-element.41.rows_ref, bf16[128,1024]{1,0:T(8,128)(2,1)S(1)} %get-tuple-element.42.scale_ref), custom_call_target="tpu_custom_call" | custom-call | flops 1000000 | bytes 1000000 | tf_op jit(solution)/shard_map/pallas_call | solution.py:512
  75.9 17.7 %all_to_all.34 = s16[128,4,128]{2,1,0:T(4,128)(2,1)S(1)} all-to-all(s16[128,4,128]{2,1,0:T(4,128)(2,1)S(1)} %bitcast.19), channel_id=1, replica_groups=mesh['rows'=128,'cols'=4] {'rows'}, dimensions={0} | all-to-all | bytes 262144 | tf_op jit(solution)/shard_map/all_to_all | solution.py:532
  93.7 0.4 shard_map.99
  94.1 10.8 %all_to_all.35.spread_ref = s16[4,336,128]{2,1,0:T(8,128)(2,1)S(1)} all-to-all(s16[4,336,128]{2,1,0:T(8,128)(2,1)S(1)} %get-tuple-element.44), channel_id=1, replica_groups=mesh['rows'=128,'cols'=4] {'cols'}, dimensions={0} | all-to-all | bytes 688128 | tf_op jit(solution)/shard_map/all_to_all | solution.py:615
  104.8 6.0 %shard_map.100 = (f32[256,128]{1,0:T(8,128)}, f32[80,256]{1,0:T(8,128)}, f32[80,256]{1,0:T(8,128)}) custom-call(s16[4,336,128]{2,1,0:T(8,128)(2,1)S(1)} %all_to_all.35.spread_ref, bf16[256,256]{1,0:T(8,128)(2,1)S(1)} %get-tuple-element.45.order_ref, bf16[128,640]{1,0:T(8,128)(2,1)S(1)} %get-tuple-element.46.leaf_scale_ref, ...), custom_call_target="tpu_custom_call" | custom-call | flops 1000000 | bytes 1000000 | tf_op jit(solution)/shard_map/pallas_call | solution.py:512
  (3 shorter events, 0.0 us)
Async XLA Ops:
  2.5 18.5 %copy-start.5 = (s32[1,4,4]{2,1,0:T(4,128)S(1)}, s32[1,4,4]{2,1,0:T(4,128)}, u32[]{:S(2)}) copy-start(s32[1,4,4]{2,1,0:T(4,128)} %param.10) | copy-start | bytes 196
  2.5 29.8 %all-to-all-start = ((s32[128,1,128]{2,1,0:T(1,128)}), s32[128,1,128]{2,1,0:T(1,128)S(1)}, u32[]{:S(2)}, u32[]{:S(2)}) async-start(s32[128,1,128]{2,1,0:T(1,128)} %bitcast.2), calls=%async_computation | async-start | bytes 131072 | tf_op jit(solution)/shard_map/all_to_all | solution.py:532
  20.9 0.7 copy-start.3
  20.9 0.7 copy-start.4
  21.0 0.7 copy-start.6
  21.6 1.0 copy-start
  22.7 9.6 %copy-start.1 = (bf16[256,80]{0,1:T(8,128)(2,1)S(1)}, bf16[256,80]{0,1:T(8,128)(2,1)}, u32[]{:S(2)}) copy-start(bf16[256,80]{0,1:T(8,128)(2,1)} %param.7) | copy-start | bytes 122884
  22.7 9.6 %copy-start.2 = (bf16[256,80]{0,1:T(8,128)(2,1)S(1)}, bf16[256,80]{0,1:T(8,128)(2,1)}, u32[]{:S(2)}) copy-start(bf16[256,80]{0,1:T(8,128)(2,1)} %param.8) | copy-start | bytes 122884

commit v8 on v7

--- a/solution.py
+++ b/solution.py
@@ -9,6 +9,7 @@
 CAP = 6
 HALF = 80
 CODES = 64
+AHEAD = 2
 LOG2 = 0.6931471805599453
 F32 = jnp.float32
 BF16 = jnp.bfloat16
@@ -438,13 +439,14 @@
             picked = jnp.where(sub == q, new[q], picked)
         lower.append(jnp.where(lane < k + b, left, 0.0))
         solved.append(jnp.where(lane < k + b, picked, 0.0))
-        if g + 1 < n // b:
-            terms = [spread(a[g + 1][:, k + q : k + q + 1]) * new[q] for q in range(b)]
+        behind = min(g + 1 + AHEAD, n // b)
+        for i in range(g + 1, behind):
+            terms = [spread(a[i][:, k + q : k + q + 1]) * new[q] for q in range(b)]
             while len(terms) > 1:
                 terms = [terms[t] + terms[t + 1] for t in range(0, len(terms), 2)]
-            a[g + 1] = jnp.where(inside, 0.0, a[g + 1]) - terms[0]
-        if g + 2 < n // b:
-            x0, x1, x2 = split3(jnp.concatenate(a[g + 2 :], axis=0))
+            a[i] = jnp.where(inside, 0.0, a[i]) - terms[0]
+        if behind < n // b:
+            x0, x1, x2 = split3(jnp.concatenate(a[behind:], axis=0))
             y0, y1, y2 = split3(
                 jnp.concatenate([picked if i == g else zero for i in range(n // b)], axis=0)
             )
@@ -452,8 +454,8 @@
                 jnp.concatenate([x0, x0, x0, x1, x1, x2], axis=1),
                 jnp.concatenate([y0, y1, y2, y0, y1, y0], axis=0),
             )
-            for i in range(g + 2, n // b):
-                first = b * (i - g - 2)
+            for i in range(behind, n // b):
+                first = b * (i - behind)
                 a[i] = jnp.where(inside, 0.0, a[i]) - change[first : first + b]
     lower = jnp.transpose(jnp.concatenate(lower, axis=0))
     return mm_full(split3(lower), split3(jnp.concatenate(solved, axis=0)))

time: 111 us -> 111 us (level)
  no operation moved by 1% of the time
where the time goes in v8:
time: 111 us
  blocking collectives  69.2 us (62%)
  starting transfers between devices  18.4 us (17%)
  Pallas kernels  12.1 us (11%)
  waiting for transfers between devices  8.37 us (8%)
  local copies, waits for them, and re-layouts  1.72 us (2%)
    all_to_all x3, blocking collectives, exchange(): return lax.all_to_all(x, 'rows', split_axis=0, concat_axis=0, tiled=True)  58.4 us
    all_to_all x1, starting transfers between devices, exchange(): return lax.all_to_all(x, 'rows', split_axis=0, concat_axis=0, tiled=True)  18.4 us
    pallas_call x7, Pallas kernels, call(): pl.pallas_call(kernel, out_shape=outs, in_specs=spec, out_specs=jax.tree....  12.1 us
    all_to_all x1, blocking collectives, per_device(): lax.all_to_all(packed, 'cols', split_axis=0, concat_axis=0, tiled=True)  10.8 us
    all_to_all x1, waiting for transfers between devices, exchange(): return lax.all_to_all(x, 'rows', split_axis=0, concat_axis=0, tiled=True)  8.37 us
  transfers between devices with their start and end apart: 1, of which 1 were waited for; matrix products, arithmetic and copies ran while one was open for 0% of the time, Pallas kernels for 1%

profile of v8, /device:TPU:1, one launch (start us, length us, event | category | flops | bytes accessed | tf_op | source)
XLA Modules:
  0.0 110.6 jit_solution(17324933008739541097)
XLA Ops:
  0.6 1.8 %shard_map.94 = s32[128,128]{1,0:T(8,128)} custom-call(s32[1,512]{1,0:T(1,128)} %targets_ref.1, s32[1,256]{1,0:T(1,128)} %bitcast.22), custom_call_target="tpu_custom_call" | custom-call | flops 1000000 | bytes 1000000 | tf_op jit(solution)/shard_map/pallas_call | solution.py:514
  2.5 0.0 copy-start.5
  2.5 18.4 %all-to-all-start = ((s32[128,1,128]{2,1,0:T(1,128)}), s32[128,1,128]{2,1,0:T(1,128)S(1)}, u32[]{:S(2)}, u32[]{:S(2)}) async-start(s32[128,1,128]{2,1,0:T(1,128)} %bitcast.2), calls=%async_computation | async-start | bytes 131072 | tf_op jit(solution)/shard_map/all_to_all | solution.py:534
  20.9 0.0 copy-start.3
  20.9 0.0 copy-start.4
  21.0 0.0 copy-start.6
  21.0 0.0 copy-done.5
  21.0 0.6 copy-done.3
  21.6 0.0 copy-done.4
  21.6 0.0 copy-done.6
  21.6 1.0 copy-done
  22.7 1.3 %shard_map.95 = (bf16[768,512]{1,0:T(8,128)(2,1)S(1)}, bf16[128,512]{1,0:T(8,128)(2,1)S(1)}, f32[8,512]{1,0:T(8,128)S(1)}, bf16[512,512]{1,0:T(8,128)(2,1)S(1)},...) custom-call(s32[1,512]{1,0:T(1,128)S(1)} %copy-done.3, ...), custom_call_target="tpu_custom_call" | custom-call | flops 1000000 | bytes 1000000 | tf_op jit(solution)/shard_map/pallas_call | solution.py:514
  23.9 8.4 %all-to-all-done = s32[128,1,128]{2,1,0:T(1,128)S(1)} async-done(((s32[128,1,128]{2,1,0:T(1,128)}), s32[128,1,128]{2,1,0:T(1,128)S(1)}, u32[]{:S(2)}, u32[]{:S(2)}) %all-to-all-start) | async-done | bytes 65568 | tf_op jit(solution)/shard_map/all_to_all | solution.py:534
  32.3 0.0 copy-done.1
  32.3 0.0 copy-done.2
  32.3 0.4 shard_map.96
  32.8 20.5 %all_to_all.32.fetched_ref = bf16[128,8,128]{2,1,0:T(8,128)(2,1)S(1)} all-to-all(bf16[128,8,128]{2,1,0:T(8,128)(2,1)S(1)} %shard_map.96), channel_id=1, replica_groups=mesh['rows'=128,'cols'=4] {'rows'}, dimensions={0} | all-to-all | bytes 524288 | tf_op jit(solution)/shard_map/all_to_all | solution.py:534
  53.2 1.2 %shard_map.97 = s16[128,8,128]{2,1,0:T(8,128)(2,1)S(1)} custom-call(bf16[128,8,128]{2,1,0:T(8,128)(2,1)S(1)} %all_to_all.32.fetched_ref, bf16[768,512]{1,0:T(8,128)(2,1)S(1)} %get-tuple-element.37.slots_ref, bf16[128,512]{1,0:T(8,128)(2,1)S(1)} %get-tuple-element.38.member_ref, f32[8,512]{1,0:T(8,128)S(1)} %get-tuple-element.39.rank_ref, ...), custom_call_target="tpu_custom_call" | custom-call | flops 1000000 | bytes 1000000 | tf_op jit(solution)/shard_map/pallas_call | solution.py:514
  54.4 20.3 %all_to_all.33.incoming_ref = s16[128,8,128]{2,1,0:T(8,128)(2,1)S(1)} all-to-all(s16[128,8,128]{2,1,0:T(8,128)(2,1)S(1)} %shard_map.97), channel_id=1, replica_groups=mesh['rows'=128,'cols'=4] {'rows'}, dimensions={0} | all-to-all | bytes 524288 | tf_op jit(solution)/shard_map/all_to_all | solution.py:534
  74.7 1.2 %shard_map.98 = s16[512,128]{1,0:T(8,128)(2,1)S(1)} custom-call(s16[128,8,128]{2,1,0:T(8,128)(2,1)S(1)} %all_to_all.33.incoming_ref, s32[128,128]{1,0:T(8,128)S(1)} %bitcast.14, s32[128,128]{1,0:T(8,128)S(1)} %get-tuple-element.41.rows_ref, bf16[128,1024]{1,0:T(8,128)(2,1)S(1)} %get-tuple-element.42.scale_ref), custom_call_target="tpu_custom_call" | custom-call | flops 1000000 | bytes 1000000 | tf_op jit(solution)/shard_map/pallas_call | solution.py:514
  75.9 17.7 %all_to_all.34 = s16[128,4,128]{2,1,0:T(4,128)(2,1)S(1)} all-to-all(s16[128,4,128]{2,1,0:T(4,128)(2,1)S(1)} %bitcast.19), channel_id=1, replica_groups=mesh['rows'=128,'cols'=4] {'rows'}, dimensions={0} | all-to-all | bytes 262144 | tf_op jit(solution)/shard_map/all_to_all | solution.py:534
  93.7 0.4 shard_map.99
  94.1 10.8 %all_to_all.35.spread_ref = s16[4,336,128]{2,1,0:T(8,128)(2,1)S(1)} all-to-all(s16[4,336,128]{2,1,0:T(8,128)(2,1)S(1)} %get-tuple-element.44), channel_id=1, replica_groups=mesh['rows'=128,'cols'=4] {'cols'}, dimensions={0} | all-to-all | bytes 688128 | tf_op jit(solution)/shard_map/all_to_all | solution.py:617
  104.8 5.7 %shard_map.100 = (f32[256,128]{1,0:T(8,128)}, f32[80,256]{1,0:T(8,128)}, f32[80,256]{1,0:T(8,128)}) custom-call(s16[4,336,128]{2,1,0:T(8,128)(2,1)S(1)} %all_to_all.35.spread_ref, bf16[256,256]{1,0:T(8,128)(2,1)S(1)} %get-tuple-element.45.order_ref, bf16[128,640]{1,0:T(8,128)(2,1)S(1)} %get-tuple-element.46.leaf_scale_ref, ...), custom_call_target="tpu_custom_call" | custom-call | flops 1000000 | bytes 1000000 | tf_op jit(solution)/shard_map/pallas_call | solution.py:514
  (3 shorter events, 0.0 us)
Async XLA Ops:
  2.5 18.5 %copy-start.5 = (s32[1,4,4]{2,1,0:T(4,128)S(1)}, s32[1,4,4]{2,1,0:T(4,128)}, u32[]{:S(2)}) copy-start(s32[1,4,4]{2,1,0:T(4,128)} %param.10) | copy-start | bytes 196
  2.5 29.8 %all-to-all-start = ((s32[128,1,128]{2,1,0:T(1,128)}), s32[128,1,128]{2,1,0:T(1,128)S(1)}, u32[]{:S(2)}, u32[]{:S(2)}) async-start(s32[128,1,128]{2,1,0:T(1,128)} %bitcast.2), calls=%async_computation | async-start | bytes 131072 | tf_op jit(solution)/shard_map/all_to_all | solution.py:534
  20.9 0.7 copy-start.3
  20.9 0.7 copy-start.4
  21.0 0.7 copy-start.6
  21.6 1.0 copy-start
  22.7 9.6 %copy-start.1 = (bf16[256,80]{0,1:T(8,128)(2,1)S(1)}, bf16[256,80]{0,1:T(8,128)(2,1)}, u32[]{:S(2)}) copy-start(bf16[256,80]{0,1:T(8,128)(2,1)} %param.7) | copy-start | bytes 122884
  22.7 9.6 %copy-start.2 = (bf16[256,80]{0,1:T(8,128)(2,1)S(1)}, bf16[256,80]{0,1:T(8,128)(2,1)}, u32[]{:S(2)}) copy-start(bf16[256,80]{0,1:T(8,128)(2,1)} %param.8) | copy-start | bytes 122884
